TPU v7x, 32 devices: a whole 2x2x4 slice. The times are simulated.
32 devices in a mesh: seq: 4 (over y, x), dp: 8 (over z, core).
Axes of the slice: x: 2, y: 2, z: 4, core: 2. Of those that a mesh axis runs over, the one named last changes fastest.
Arguments:
- hidden_in: bfloat16 [16, 1024, 1024], P('dp', 'seq'), may hold values from -6 to 6
- documents: int32 [16, 1024], P('dp'), may hold values from 0 to 2, as said below
- cotangent: bfloat16 [16, 1024, 1024], P('dp', 'seq'), may hold values from -6 to 6
- mixer_gain: bfloat16 [1024], P(('seq', 'dp')), may hold values from 0.5 to 1.5
- mamba_gate: bfloat16 [1024, 1536], P(('seq', 'dp')), may hold values from -0.1875 to 0.1875
- mamba_input: bfloat16 [1024, 1792], P(('seq', 'dp')), may hold values from -0.1875 to 0.1875
- step_weight: bfloat16 [1024, 24], P(('seq', 'dp')), may hold values from -0.1875 to 0.1875
- conv_taps: bfloat16 [4, 1792], P(None, ('seq', 'dp')), may hold values from -3 to 3
- conv_bias: bfloat16 [1792], P(('seq', 'dp')), may hold values from -3 to 3
- step_bias: float32 [24], replicated, may hold values from -7 to -3
- decay_log: float32 [24], replicated, may hold values from -1 to 1.5
- skip_scale: float32 [24], replicated, may hold values from 0.5 to 1.5
- mamba_gain: bfloat16 [1536], P(('seq', 'dp')), may hold values from 0.5 to 1.5
- mamba_output: bfloat16 [1536, 1024], P(('seq', 'dp')), may hold values from -0.15625 to 0.15625
- query_weight: bfloat16 [1024, 512], P(('seq', 'dp')), may hold values from -0.1875 to 0.1875
- keyvalue_matrix: bfloat16 [1024, 256], P(('seq', 'dp')), may hold values from -0.1875 to 0.1875
- attn_output: bfloat16 [512, 1024], P(('seq', 'dp')), may hold values from -3 to 3
- ffn_gain: bfloat16 [1024], P(('seq', 'dp')), may hold values from 0.5 to 1.5
- gate_up: bfloat16 [1024, 4096], P(('seq', 'dp')), may hold values from -0.1875 to 0.1875
- down_weight: bfloat16 [2048, 1024], P(('seq', 'dp')), may hold values from -0.125 to 0.125
Outputs:
- layer_out: bfloat16 [16, 1024, 1024], P('dp', 'seq')
- grad_input: bfloat16 [16, 1024, 1024], P('dp', 'seq')
- grad_mixer_gain: float32 [1024], P(('seq', 'dp'))
- grad_mamba_gate: float32 [1024, 1536], P(('seq', 'dp'))
- grad_mamba_input: float32 [1024, 1792], P(('seq', 'dp'))
- grad_step_weight: float32 [1024, 24], P(('seq', 'dp'))
- grad_conv_taps: float32 [4, 1792], P(None, ('seq', 'dp'))
- grad_conv_bias: float32 [1792], P(('seq', 'dp'))
- grad_step_bias: float32 [24], replicated
- grad_decay_log: float32 [24], replicated
- grad_skip_scale: float32 [24], replicated
- grad_mamba_gain: float32 [1536], P(('seq', 'dp'))
- grad_mamba_output: float32 [1536, 1024], P(('seq', 'dp'))
- grad_query_weight: float32 [1024, 512], P(('seq', 'dp'))
- grad_keyvalue_weight: float32 [1024, 256], P(('seq', 'dp'))
- grad_attn_output: float32 [512, 1024], P(('seq', 'dp'))
- grad_ffn_gain: float32 [1024], P(('seq', 'dp'))
- grad_gate_up: float32 [1024, 4096], P(('seq', 'dp'))
- grad_down_weight: float32 [2048, 1024], P(('seq', 'dp'))
Inputs may be any that keep to these rules, and one draw needn't show every extreme that they name: Each row holds documents 0, 1, 2 in order: document 0 has 1 to 128 tokens at the row's start, document 2 has 1 to 128 tokens at its end, document 1 the rest.
All inputs are finite; a program needn't handle non-finite values.
Results may differ from a plain program's by a relative error of at most 0.014.
Values may be sent and summed in bfloat16 or wider, within the bound.
A program may use at most 256 MiB of HBM per device.

v0:
```python
import jax
import jax.numpy as jnp
from jax import lax
from jax.sharding import PartitionSpec as P

QUERY_HEADS = 8
KEYVALUE_HEADS = 2
HEAD_SIZE = 64


EPSILON = 1e-05
THETA_BASE = 100000000000.0
TOP_PRECISION = lax.Precision.HIGHEST


def passed_along(block, axis, distance):
    devices = range(lax.axis_size(axis))
    route = [(i - distance, i) for i in devices if i - distance in devices]
    return lax.ppermute(block, axis, route)


def prefix(value, axis, join, neutral):
    count, mine = (lax.axis_size(axis), lax.axis_index(axis))
    pieces = jax.tree.map(lambda part: lax.all_gather(part, axis), value)
    total = jax.tree.map(
        lambda part, zero: jnp.full_like(part, 0) + jnp.asarray(zero, part.dtype), value, neutral
    )

    def prefix_step(position, total):
        longer = join(total, jax.tree.map(lambda part: part[position], pieces))
        return jax.tree.map(lambda new, old: jnp.where(position < mine, new, old), longer, total)

    return lax.fori_loop(0, count - 1, prefix_step, total)


def carried_in_2(x, axis, combine, identity):
    peers, place = (lax.axis_size(axis), lax.axis_index(axis))
    everything = jax.tree.map(
        lambda part, kind: lax.all_gather(part.astype(kind), axis),
        x,
        jax.tree.map(lambda a: jnp.bfloat16 if a.dtype == jnp.float32 else a.dtype, x),
    )
    start = jax.tree.map(
        lambda part, zero: jnp.broadcast_to(jnp.asarray(zero, part.dtype), part.shape), x, identity
    )

    def carried_step(k, before):
        at = peers - 1 - k
        reached = at > place
        new = combine(
            before, jax.tree.map(lambda part, own: part[at].astype(own.dtype), everything, x)
        )
        return jax.tree.map(lambda a, b: jnp.where(reached, a, b), new, before)

    return lax.fori_loop(0, peers, carried_step, start)


def product(left_side, right_side):
    return jnp.dot(left_side, right_side, preferred_element_type=jnp.float32)


def product_tn(left_side, right_side):
    return lax.dot_general(
        left_side, right_side, (((0,), (0,)), ((), ())), preferred_element_type=jnp.float32
    )


def product_nt(left_side, right_side):
    return lax.dot_general(
        left_side, right_side, (((1,), (1,)), ((), ())), preferred_element_type=jnp.float32
    )


def silu_slope(values):
    sigma = jax.nn.sigmoid(values)
    return sigma * (1.0 + values * (1.0 - sigma))


def norm_back(values, inverse, grad_out):
    return inverse * grad_out - values * inverse**3 * jnp.mean(
        grad_out * values, axis=-1, keepdims=True
    )


def chain_link(earlier, later_one):
    return (earlier[0] * later_one[0], later_one[0][..., None, None] * earlier[1] + later_one[1])


def rotate(values, places):
    head_view = values.reshape(values.shape[0], -1, HEAD_SIZE)
    half_head = HEAD_SIZE // 2
    frequencies = jnp.exp(
        -jnp.log(THETA_BASE) * jnp.arange(half_head, dtype=jnp.float32) / half_head
    )
    angles = places[:, None] * frequencies[None, :]
    cosine = jnp.cos(angles)[:, None, :]
    sine_vals = jnp.sin(angles)[:, None, :]
    first_half = head_view[:, :, :half_head]
    second_half = head_view[:, :, half_head:]
    turned = jnp.concatenate(
        [
            first_half * cosine - second_half * sine_vals,
            second_half * cosine + first_half * sine_vals,
        ],
        axis=2,
    )
    return turned.reshape(values.shape)


def conv_apply(padded, doc_padded, doc_seq, taps, bias):
    count_rows = doc_seq.shape[0]
    summed = jnp.zeros((count_rows, padded.shape[1]), jnp.float32) + bias[None, :]
    for tap_index in range(taps.shape[0]):
        window = padded[tap_index : tap_index + count_rows]
        matched = doc_padded[tap_index : tap_index + count_rows] == doc_seq
        summed = summed + jnp.where(matched[:, None], window, 0.0) * taps[tap_index][None, :]
    return summed


def piece_carry(xs_piece, b_piece, step_piece, log_piece, doc_piece, prev_doc):
    cumulative = jnp.cumsum(log_piece, axis=0)
    at_end = (doc_piece == doc_piece[-1])[:, None]
    weights = jnp.where(at_end, jnp.exp(cumulative[-1][None, :] - cumulative), 0.0) * step_piece
    states = jnp.einsum("qh,qhp,qn->hpn", weights, xs_piece, b_piece, precision=TOP_PRECISION)
    decays = jnp.where(doc_piece[-1] == prev_doc, jnp.exp(cumulative[-1]), 0.0)
    return (decays, states)


def piece_output(
    xs_piece, b_piece, c_piece, step_piece, log_piece, doc_piece, prev_doc, carried, skip_scale
):
    cumulative = jnp.cumsum(log_piece, axis=0)
    local_rows = log_piece.shape[0]
    row_index = lax.broadcasted_iota(jnp.int32, (local_rows, local_rows), 0)
    col_index = lax.broadcasted_iota(jnp.int32, (local_rows, local_rows), 1)
    linked = (row_index >= col_index) & (doc_piece[:, None] == doc_piece[None, :])
    spread = cumulative.T[:, :, None] - cumulative.T[:, None, :]
    factors = jnp.where(linked[None], jnp.exp(jnp.where(linked[None], spread, 0.0)), 0.0)
    inner_prod = jnp.dot(
        c_piece, b_piece.T, precision=TOP_PRECISION, preferred_element_type=jnp.float32
    )
    mixing = factors * inner_prod[None] * step_piece.T[:, None, :]
    result = jnp.einsum("hts,shp->thp", mixing, xs_piece, precision=TOP_PRECISION)
    entering = jnp.where((doc_piece == prev_doc)[:, None], jnp.exp(cumulative), 0.0)
    from_state = jnp.einsum("tn,hpn->thp", c_piece, carried, precision=TOP_PRECISION)
    return result + entering[:, :, None] * from_state + skip_scale[None, :, None] * xs_piece


def score_block(query_row_block, keyvalue_rows, doc_query, doc_keys, query_places):
    local_rows = query_row_block.shape[0]
    local_keys = keyvalue_rows.shape[0]
    key_span_width = KEYVALUE_HEADS * HEAD_SIZE
    query_head_rows = query_row_block.reshape(
        local_rows, KEYVALUE_HEADS, QUERY_HEADS // KEYVALUE_HEADS, HEAD_SIZE
    )
    key_head_rows = keyvalue_rows[:, :key_span_width].reshape(local_keys, KEYVALUE_HEADS, HEAD_SIZE)
    score_matrix = jnp.einsum(
        "lbon,ybn->boly", query_head_rows, key_head_rows, preferred_element_type=jnp.float32
    ) * HEAD_SIZE ** (-0.5)
    allowed = (query_places[:, None] >= jnp.arange(local_keys)[None, :]) & (
        doc_query[:, None] == doc_keys[None, :]
    )
    return jnp.where(allowed[None, None], score_matrix, -1e30)


def attend_forward(query_row_block, keyvalue_rows, doc_query, doc_keys, query_places):
    local_rows = query_row_block.shape[0]
    local_keys = keyvalue_rows.shape[0]
    key_span_width = KEYVALUE_HEADS * HEAD_SIZE
    masked = score_block(query_row_block, keyvalue_rows, doc_query, doc_keys, query_places)
    row_peak = jnp.max(masked, axis=-1, keepdims=True)
    exp_scores = jnp.exp(masked - row_peak)
    row_total = jnp.sum(exp_scores, axis=-1, keepdims=True)
    softmax_row_block = (exp_scores / row_total).astype(jnp.bfloat16)
    value_head_rows = keyvalue_rows[:, key_span_width:].reshape(
        local_keys, KEYVALUE_HEADS, HEAD_SIZE
    )
    merged_heads = jnp.einsum(
        "vyka,avo->kvyo", softmax_row_block, value_head_rows, preferred_element_type=jnp.float32
    )
    return (
        merged_heads.reshape(local_rows, QUERY_HEADS * HEAD_SIZE),
        row_peak + jnp.log(row_total),
    )


def attend_backward(
    query_row_block, keyvalue_rows, doc_query, doc_keys, query_places, log_norm, mixed_gradient
):
    local_rows = query_row_block.shape[0]
    local_keys = keyvalue_rows.shape[0]
    key_span_width = KEYVALUE_HEADS * HEAD_SIZE
    masked = score_block(query_row_block, keyvalue_rows, doc_query, doc_keys, query_places)
    softmax_row_block = jnp.exp(masked - log_norm)
    query_head_rows = query_row_block.reshape(
        local_rows, KEYVALUE_HEADS, QUERY_HEADS // KEYVALUE_HEADS, HEAD_SIZE
    )
    key_head_rows = keyvalue_rows[:, :key_span_width].reshape(local_keys, KEYVALUE_HEADS, HEAD_SIZE)
    value_head_rows = keyvalue_rows[:, key_span_width:].reshape(
        local_keys, KEYVALUE_HEADS, HEAD_SIZE
    )
    heads_gradient = mixed_gradient.reshape(
        local_rows, KEYVALUE_HEADS, QUERY_HEADS // KEYVALUE_HEADS, HEAD_SIZE
    )
    grad_probs = jnp.einsum(
        "lbon,ybn->boly", heads_gradient, value_head_rows, preferred_element_type=jnp.float32
    )
    centre = jnp.sum(softmax_row_block * grad_probs, axis=-1, keepdims=True)
    scores_gradient = (softmax_row_block * (grad_probs - centre)).astype(jnp.bfloat16)
    grad_query = jnp.einsum(
        "vyka,avo->kvyo", scores_gradient, key_head_rows, preferred_element_type=jnp.float32
    ) * HEAD_SIZE ** (-0.5)
    grad_key = jnp.einsum(
        "ncuy,uncp->ynp", scores_gradient, query_head_rows, preferred_element_type=jnp.float32
    ) * HEAD_SIZE ** (-0.5)
    grad_value = jnp.einsum(
        "ncuy,uncp->ynp",
        softmax_row_block.astype(jnp.bfloat16),
        heads_gradient,
        preferred_element_type=jnp.float32,
    )
    grad_keyval = jnp.concatenate(
        [
            grad_key.reshape(local_keys, key_span_width),
            grad_value.reshape(local_keys, key_span_width),
        ],
        axis=1,
    )
    return (grad_query.reshape(local_rows, QUERY_HEADS * HEAD_SIZE), grad_keyval)


def local(
    hidden_in,
    documents,
    cotangent,
    mixer_gain,
    mamba_gate,
    mamba_input,
    step_weight,
    conv_taps,
    conv_bias,
    step_bias,
    decay_log,
    skip_scale,
    mamba_gain,
    mamba_output,
    query_weight,
    keyvalue_matrix,
    attn_output,
    ffn_gain,
    gate_up,
    down_weight,
):
    seq_count, piece_len, model_width = hidden_in.shape
    seq_rank = lax.axis_index("seq")
    first_row = seq_rank * piece_len
    (
        gain_one,
        gate_full,
        input_full,
        step_full,
        taps_full,
        bias_full,
        gain_mamba,
        output_full,
        query_full,
        keyvalue_full,
        attn_full,
    ) = (
        lax.all_gather(mixer_gain, ("seq", "dp"), axis=0, tiled=True),
        lax.all_gather(mamba_gate, ("seq", "dp"), axis=0, tiled=True),
        lax.all_gather(mamba_input, ("seq", "dp"), axis=0, tiled=True),
        lax.all_gather(step_weight, ("seq", "dp"), axis=0, tiled=True),
        lax.all_gather(conv_taps, ("seq", "dp"), axis=1, tiled=True),
        lax.all_gather(conv_bias, ("seq", "dp"), axis=0, tiled=True),
        lax.all_gather(mamba_gain, ("seq", "dp"), axis=0, tiled=True),
        lax.all_gather(mamba_output, ("seq", "dp"), axis=0, tiled=True),
        lax.all_gather(query_weight, ("seq", "dp"), axis=0, tiled=True),
        lax.all_gather(keyvalue_matrix, ("seq", "dp"), axis=0, tiled=True),
        lax.all_gather(attn_output, ("seq", "dp"), axis=0, tiled=True),
    )
    rim_width = taps_full.shape[0] - 1
    doc_own = lax.dynamic_slice_in_dim(documents, first_row, piece_len, 1)
    doc_rim = lax.dynamic_slice_in_dim(
        documents, jnp.maximum(first_row - rim_width, 0), rim_width, 1
    )
    doc_rim = jnp.where(seq_rank > 0, doc_rim, -1)
    prev_doc = doc_rim[:, -1]
    flat_rows = hidden_in.reshape(-1, model_width).astype(jnp.float32)
    inv_one = lax.rsqrt(jnp.mean(flat_rows * flat_rows, axis=-1, keepdims=True) + EPSILON)
    gain_first = gain_one.astype(jnp.float32)
    normed = (flat_rows * inv_one * gain_first).astype(jnp.bfloat16)
    gate_pre = product(normed, gate_full)
    conv_in = product(normed, input_full).astype(jnp.bfloat16)
    step_raw = product(normed, step_full)
    query_raw = product(normed, query_full)
    keyvalue_raw = product(normed, keyvalue_full)
    conv_width = conv_in.shape[1]
    conv_seq = conv_in.reshape(seq_count, piece_len, conv_width)
    rim_rows = passed_along(conv_seq[:, piece_len - rim_width :, :], "seq", 1)
    padded = jnp.concatenate([rim_rows, conv_seq], axis=1).astype(jnp.float32)
    doc_padded = jnp.concatenate([doc_rim, doc_own], axis=1)

    def conv_fn(pad_in, taps_in, bias_in):
        return jax.vmap(conv_apply, in_axes=(0, 0, 0, None, None))(
            pad_in, doc_padded, doc_own, taps_in, bias_in
        )

    conv_out, conv_pull = jax.vjp(
        conv_fn, padded, taps_full.astype(jnp.float32), bias_full.astype(jnp.float32)
    )
    conv_act = jax.nn.silu(conv_out).astype(jnp.bfloat16)
    ssm_width = gate_pre.shape[1]
    heads_ssm = step_raw.shape[1]
    state_width = (conv_width - ssm_width) // 2
    act_float = conv_act.astype(jnp.float32)
    xs_all = act_float[:, :, :ssm_width].reshape(
        seq_count, piece_len, heads_ssm, ssm_width // heads_ssm
    )
    b_all = act_float[:, :, ssm_width : ssm_width + state_width]
    c_all = act_float[:, :, ssm_width + state_width :]
    step_sum = step_raw + step_bias[None, :]
    steps_dt = jax.nn.softplus(step_sum)
    rates = jnp.exp(decay_log)
    log_decay = -steps_dt * rates[None, :]
    step_seq = steps_dt.reshape(seq_count, piece_len, heads_ssm)
    log_seq = log_decay.reshape(seq_count, piece_len, heads_ssm)

    def carry_fn(xs_in, b_in, step_in, log_in):
        return jax.vmap(piece_carry)(xs_in, b_in, step_in, log_in, doc_own, prev_doc)

    (decays, states), carry_pull = jax.vjp(carry_fn, xs_all, b_all, step_seq, log_seq)
    entered = prefix(
        (decays, states), "seq", chain_link, (jnp.ones_like(decays), jnp.zeros_like(states))
    )[1]

    def output_fn(xs_in, b_in, c_in, step_in, log_in, carried_in, skip_in):
        return jax.vmap(piece_output, in_axes=(0, 0, 0, 0, 0, 0, 0, 0, None))(
            xs_in, b_in, c_in, step_in, log_in, doc_own, prev_doc, carried_in, skip_in
        )

    ssm_out, output_pull = jax.vjp(
        output_fn, xs_all, b_all, c_all, step_seq, log_seq, entered, skip_scale
    )
    ssm_flat = ssm_out.reshape(-1, ssm_width)
    gate_act = jax.nn.silu(gate_pre)
    gated_rows = ssm_flat * gate_act
    inv_mamba = lax.rsqrt(jnp.mean(gated_rows * gated_rows, axis=-1, keepdims=True) + EPSILON)
    gain_second_m = gain_mamba.astype(jnp.float32)
    mamba_norm = (gated_rows * inv_mamba * gain_second_m).astype(jnp.bfloat16)
    mamba_branch = product(mamba_norm, output_full)
    query_places = first_row + jnp.arange(piece_len, dtype=jnp.int32)
    places = jnp.tile(query_places.astype(jnp.float32), seq_count)
    key_span_width = keyvalue_raw.shape[1] // 2
    query_block = rotate(query_raw, places).astype(jnp.bfloat16)
    keyvalue_pairs = jnp.concatenate(
        [rotate(keyvalue_raw[:, :key_span_width], places), keyvalue_raw[:, key_span_width:]], axis=1
    ).astype(jnp.bfloat16)
    kv_whole = lax.all_gather(
        keyvalue_pairs.reshape(seq_count, piece_len, 2 * key_span_width), "seq", axis=1, tiled=True
    )
    query_seq = query_block.reshape(seq_count, piece_len, -1)
    attn_mix, log_norm = jax.vmap(attend_forward, in_axes=(0, 0, 0, 0, None))(
        query_seq, kv_whole, doc_own, documents, query_places
    )
    attn_rows = attn_mix.reshape(seq_count * piece_len, -1).astype(jnp.bfloat16)
    attn_branch = product(attn_rows, attn_full)
    mixed_rows = flat_rows + mamba_branch + attn_branch
    gain_two, gate_up_full, down_full = (
        lax.all_gather(ffn_gain, ("seq", "dp"), axis=0, tiled=True),
        lax.all_gather(gate_up, ("seq", "dp"), axis=0, tiled=True),
        lax.all_gather(down_weight, ("seq", "dp"), axis=0, tiled=True),
    )
    inv_two = lax.rsqrt(jnp.mean(mixed_rows * mixed_rows, axis=-1, keepdims=True) + EPSILON)
    gain_second = gain_two.astype(jnp.float32)
    normed_two = (mixed_rows * inv_two * gain_second).astype(jnp.bfloat16)
    gate_up_out = product(normed_two, gate_up_full)
    hidden_units = gate_up_out.shape[1] // 2
    gate_part = gate_up_out[:, :hidden_units]
    up_part = gate_up_out[:, hidden_units:]
    gate_silu = jax.nn.silu(gate_part)
    ffn_act = (gate_silu * up_part).astype(jnp.bfloat16)
    ffn_branch = product(ffn_act, down_full)
    layer_out = (mixed_rows + ffn_branch).astype(jnp.bfloat16).reshape(hidden_in.shape)
    (
        gain_one,
        gate_full,
        input_full,
        step_full,
        taps_full,
        bias_full,
        gain_mamba,
        output_full,
        query_full,
        keyvalue_full,
        attn_full,
        gain_two,
        gate_up_full,
        down_full,
    ) = (
        lax.all_gather(mixer_gain, ("seq", "dp"), axis=0, tiled=True),
        lax.all_gather(mamba_gate, ("seq", "dp"), axis=0, tiled=True),
        lax.all_gather(mamba_input, ("seq", "dp"), axis=0, tiled=True),
        lax.all_gather(step_weight, ("seq", "dp"), axis=0, tiled=True),
        lax.all_gather(conv_taps, ("seq", "dp"), axis=1, tiled=True),
        lax.all_gather(conv_bias, ("seq", "dp"), axis=0, tiled=True),
        lax.all_gather(mamba_gain, ("seq", "dp"), axis=0, tiled=True),
        lax.all_gather(mamba_output, ("seq", "dp"), axis=0, tiled=True),
        lax.all_gather(query_weight, ("seq", "dp"), axis=0, tiled=True),
        lax.all_gather(keyvalue_matrix, ("seq", "dp"), axis=0, tiled=True),
        lax.all_gather(attn_output, ("seq", "dp"), axis=0, tiled=True),
        lax.all_gather(ffn_gain, ("seq", "dp"), axis=0, tiled=True),
        lax.all_gather(gate_up, ("seq", "dp"), axis=0, tiled=True),
        lax.all_gather(down_weight, ("seq", "dp"), axis=0, tiled=True),
    )
    grad_out = cotangent.reshape(-1, model_width).astype(jnp.float32)
    grad_ffn_branch = grad_out.astype(jnp.bfloat16)
    grad_down = product_tn(ffn_act, grad_ffn_branch)
    grad_act = product_nt(grad_ffn_branch, down_full)
    grad_gate_up_rows = jnp.concatenate(
        [grad_act * up_part * silu_slope(gate_part), grad_act * gate_silu], axis=1
    ).astype(jnp.bfloat16)
    grad_gate_up_w = product_tn(normed_two, grad_gate_up_rows)
    grad_normed_two = product_nt(grad_gate_up_rows, gate_up_full)
    grad_gain_two = jnp.sum(grad_normed_two * mixed_rows * inv_two, axis=0)
    mixed_gradient = grad_out + norm_back(mixed_rows, inv_two, grad_normed_two * gain_second)
    grad_gain_two, grad_gate_up_w, grad_down = (
        lax.psum_scatter(grad_gain_two, ("seq", "dp"), scatter_dimension=0, tiled=True),
        lax.psum_scatter(grad_gate_up_w, ("seq", "dp"), scatter_dimension=0, tiled=True),
        lax.psum_scatter(grad_down, ("seq", "dp"), scatter_dimension=0, tiled=True),
    )
    grad_branch = mixed_gradient.astype(jnp.bfloat16)
    grad_attn_w = product_tn(attn_rows, grad_branch)
    grad_attn_rows = product_nt(grad_branch, attn_full).astype(jnp.bfloat16)
    grad_mamba_out_w = product_tn(mamba_norm, grad_branch)
    grad_mamba_norm = product_nt(grad_branch, output_full)
    grad_gain_mamba = jnp.sum(grad_mamba_norm * gated_rows * inv_mamba, axis=0)
    grad_gated = norm_back(gated_rows, inv_mamba, grad_mamba_norm * gain_mamba.astype(jnp.float32))
    grad_ssm = grad_gated * gate_act
    grad_gate_pre = (grad_gated * ssm_flat * silu_slope(gate_pre)).astype(jnp.bfloat16)
    grad_q_seq, grad_kv_whole = jax.vmap(attend_backward, in_axes=(0, 0, 0, 0, None, 0, 0))(
        query_seq,
        kv_whole,
        doc_own,
        documents,
        query_places,
        log_norm,
        grad_attn_rows.reshape(seq_count, piece_len, -1),
    )
    grad_kv_own = lax.psum_scatter(
        grad_kv_whole.astype(jnp.bfloat16), "seq", scatter_dimension=1, tiled=True
    ).astype(jnp.float32)
    grad_query_raw = rotate(grad_q_seq.reshape(seq_count * piece_len, -1), -places).astype(
        jnp.bfloat16
    )
    grad_kv_flat = grad_kv_own.reshape(seq_count * piece_len, 2 * key_span_width)
    grad_keyvalue_raw = jnp.concatenate(
        [rotate(grad_kv_flat[:, :key_span_width], -places), grad_kv_flat[:, key_span_width:]],
        axis=1,
    ).astype(jnp.bfloat16)
    grad_xs_one, grad_b_one, grad_c_one, grad_step_one, grad_log_one, grad_entered, grad_skip = (
        output_pull(grad_ssm.reshape(ssm_out.shape))
    )
    leaving = carried_in_2(
        (decays, grad_entered),
        "seq",
        chain_link,
        (jnp.ones_like(decays), jnp.zeros_like(grad_entered)),
    )[1]
    grad_decays = jnp.sum(leaving * entered, axis=(2, 3))
    grad_xs_two, grad_b_two, grad_step_two, grad_log_two = carry_pull((grad_decays, leaving))
    grad_log = (grad_log_one + grad_log_two).reshape(-1, heads_ssm)
    grad_steps = (grad_step_one + grad_step_two).reshape(-1, heads_ssm) - grad_log * rates[None, :]
    grad_decay_log = jnp.sum(grad_log * log_decay, axis=0)
    grad_step_sum = grad_steps * jax.nn.sigmoid(step_sum)
    grad_step_bias = jnp.sum(grad_step_sum, axis=0)
    grad_step_raw = grad_step_sum.astype(jnp.bfloat16)
    grad_conv_act = jnp.concatenate(
        [
            (grad_xs_one + grad_xs_two).reshape(seq_count, piece_len, ssm_width),
            grad_b_one + grad_b_two,
            grad_c_one,
        ],
        axis=2,
    )
    grad_conv = grad_conv_act * silu_slope(conv_out)
    grad_padded, grad_taps, grad_conv_b = conv_pull(grad_conv)
    rim_grads = passed_along(grad_padded[:, :rim_width, :].astype(jnp.bfloat16), "seq", -1).astype(
        jnp.float32
    )
    grad_conv_in = grad_padded[:, rim_width:, :] + jnp.concatenate(
        [jnp.zeros((seq_count, piece_len - rim_width, conv_width), jnp.float32), rim_grads], axis=1
    )
    grad_conv_in = grad_conv_in.reshape(-1, conv_width).astype(jnp.bfloat16)
    grad_normed = (
        product_nt(grad_gate_pre, gate_full)
        + product_nt(grad_conv_in, input_full)
        + product_nt(grad_step_raw, step_full)
        + product_nt(grad_query_raw, query_full)
        + product_nt(grad_keyvalue_raw, keyvalue_full)
    )
    grad_gate_w = product_tn(normed, grad_gate_pre)
    grad_input_w = product_tn(normed, grad_conv_in)
    grad_step_w = product_tn(normed, grad_step_raw)
    grad_query_w = product_tn(normed, grad_query_raw)
    grad_keyvalue_w = product_tn(normed, grad_keyvalue_raw)
    grad_gain_one = jnp.sum(grad_normed * flat_rows * inv_one, axis=0)
    grad_input = (
        (mixed_gradient + norm_back(flat_rows, inv_one, grad_normed * gain_first))
        .astype(jnp.bfloat16)
        .reshape(hidden_in.shape)
    )
    (
        grad_gain_one,
        grad_gate_w,
        grad_input_w,
        grad_step_w,
        grad_taps,
        grad_conv_b,
        grad_gain_mamba,
        grad_mamba_out_w,
        grad_query_w,
        grad_keyvalue_w,
        grad_attn_w,
    ) = (
        lax.psum_scatter(grad_gain_one, ("seq", "dp"), scatter_dimension=0, tiled=True),
        lax.psum_scatter(grad_gate_w, ("seq", "dp"), scatter_dimension=0, tiled=True),
        lax.psum_scatter(grad_input_w, ("seq", "dp"), scatter_dimension=0, tiled=True),
        lax.psum_scatter(grad_step_w, ("seq", "dp"), scatter_dimension=0, tiled=True),
        lax.psum_scatter(grad_taps, ("seq", "dp"), scatter_dimension=1, tiled=True),
        lax.psum_scatter(grad_conv_b, ("seq", "dp"), scatter_dimension=0, tiled=True),
        lax.psum_scatter(grad_gain_mamba, ("seq", "dp"), scatter_dimension=0, tiled=True),
        lax.psum_scatter(grad_mamba_out_w, ("seq", "dp"), scatter_dimension=0, tiled=True),
        lax.psum_scatter(grad_query_w, ("seq", "dp"), scatter_dimension=0, tiled=True),
        lax.psum_scatter(grad_keyvalue_w, ("seq", "dp"), scatter_dimension=0, tiled=True),
        lax.psum_scatter(grad_attn_w, ("seq", "dp"), scatter_dimension=0, tiled=True),
    )
    grad_step_bias, grad_decay_log, grad_skip = lax.psum(
        (grad_step_bias, grad_decay_log, grad_skip), ("seq", "dp")
    )
    return (
        layer_out,
        grad_input,
        grad_gain_one,
        grad_gate_w,
        grad_input_w,
        grad_step_w,
        grad_taps,
        grad_conv_b,
        grad_step_bias,
        grad_decay_log,
        grad_skip,
        grad_gain_mamba,
        grad_mamba_out_w,
        grad_query_w,
        grad_keyvalue_w,
        grad_attn_w,
        grad_gain_two,
        grad_gate_up_w,
        grad_down,
    )


def solution(mesh):
    in_specs = (
        P("dp", "seq", None),
        P("dp", None),
        P("dp", "seq", None),
        P(("seq", "dp")),
        P(("seq", "dp"), None),
        P(("seq", "dp"), None),
        P(("seq", "dp"), None),
        P(None, ("seq", "dp")),
        P(("seq", "dp")),
        P(),
        P(),
        P(),
        P(("seq", "dp")),
        P(("seq", "dp"), None),
        P(("seq", "dp"), None),
        P(("seq", "dp"), None),
        P(("seq", "dp"), None),
        P(("seq", "dp")),
        P(("seq", "dp"), None),
        P(("seq", "dp"), None),
    )
    out_specs = (
        P("dp", "seq", None),
        P("dp", "seq", None),
        P(("seq", "dp")),
        P(("seq", "dp"), None),
        P(("seq", "dp"), None),
        P(("seq", "dp"), None),
        P(None, ("seq", "dp")),
        P(("seq", "dp")),
        P(),
        P(),
        P(),
        P(("seq", "dp")),
        P(("seq", "dp"), None),
        P(("seq", "dp"), None),
        P(("seq", "dp"), None),
        P(("seq", "dp"), None),
        P(("seq", "dp")),
        P(("seq", "dp"), None),
        P(("seq", "dp"), None),
    )
    return jax.shard_map(local, mesh=mesh, in_specs=in_specs, out_specs=out_specs, check_vma=False)
```

profile of v0, /device:TPU:0, one launch (start us, length us, event | category | flops | bytes accessed | tf_op | source)
XLA Modules:
  0.0 2035.8 jit_solution(14614129582014008993)
XLA Ops:
  12.9 42.3 %all-reduce.21 = (bf16[1024]{0:T(1024)(128)(2,1)S(1)}, bf16[1792]{0:T(1024)(128)(2,1)S(1)}, bf16[1536]{0:T(1024)(128)(2,1)S(1)}, bf16[1024]{0:T(1024)(128)(2,1)S(1)}) all-reduce(bf16[1024]{0:T(1024)(128)(2,1)S(1)} %dynamic-update-slice.1, bf16[1792]{0:T(1024)(128)(2,1)S(1)} %dynamic-update-slice, ...), channel_id=1, replica_groups=mesh['seq'=4,'dp'=8] {'seq','dp'}, use_global_device_ids=true, to_apply=%add.12 | all-reduce | flops 5376 | bytes 21504
  55.2 43.1 %all_gather.86 = bf16[1024,256]{1,0:T(8,128)(2,1)S(1)} all-gather(bf16[32,256]{1,0:T(8,128)(2,1)} %param.39), channel_id=1, replica_groups=mesh['seq'=4,'dp'=8] {'seq','dp'}, dimensions={0}, use_global_device_ids=true | all-gather | bytes 540672 | tf_op jit(solution)/shard_map/all_gather | solution.py:279
  104.5 36.7 %all-gather.2 = bf16[32,56,4]{1,2,0:T(4,128)(2,1)S(1)} all-gather(bf16[1,56,4]{1,2,0:T(4,128)(2,1)S(1)} %bitcast.396), channel_id=1, replica_groups=mesh['seq'=4,'dp'=8] {'seq','dp'}, dimensions={0}, use_global_device_ids=true | all-gather | bytes 14784 | tf_op jit(solution)/shard_map/all_gather | solution.py:274
  141.4 38.8 %all-gather.3 = bf16[32,32,24]{1,2,0:T(8,128)(2,1)S(1)} all-gather(bf16[1,32,24]{1,2,0:T(8,128)(2,1)S(1)} %bitcast.393), channel_id=1, replica_groups=mesh['seq'=4,'dp'=8] {'seq','dp'}, dimensions={0}, use_global_device_ids=true | all-gather | bytes 50688 | tf_op jit(solution)/shard_map/all_gather | solution.py:273
  210.9 11.8 all_gather.80
  284.6 12.3 fusion.39
  309.4 27.6 %all-gather.17.cloned.1.call-done = bf16[1024,1536]{1,0:T(8,128)(2,1)} async-done(((bf16[32,1536]{1,0:T(8,128)(2,1)}), bf16[1024,1536]{1,0:T(8,128)(2,1)}) %all-gather.17.cloned.1.call-update) | async-done | bytes 3145744 | tf_op jit(solution)/shard_map/all_gather | solution.py:271
  345.0 52.8 %all-gather.19.cloned.1.call-done = bf16[1536,1024]{1,0:T(8,128)(2,1)} async-done(((bf16[48,1024]{1,0:T(8,128)(2,1)}), bf16[1536,1024]{1,0:T(8,128)(2,1)}) %all-gather.19.cloned.1.call-update) | async-done | bytes 3145744 | tf_op jit(solution)/shard_map/all_gather | solution.py:277
  404.0 49.5 %all-gather.25.cloned.1.call-done = bf16[512,1024]{1,0:T(8,128)(2,1)} async-done(((bf16[16,1024]{1,0:T(8,128)(2,1)}), bf16[512,1024]{1,0:T(8,128)(2,1)}) %all-gather.25.cloned.1.call-update) | async-done | bytes 1048592 | tf_op jit(solution)/shard_map/all_gather | solution.py:280
  457.6 75.2 %all-gather.27.cloned.1.call-done = bf16[1024,4096]{1,0:T(8,128)(2,1)} async-done(((bf16[32,4096]{1,0:T(8,128)(2,1)}), bf16[1024,4096]{1,0:T(8,128)(2,1)}) %all-gather.27.cloned.1.call-update) | async-done | bytes 8388624 | tf_op jit(solution)/shard_map/all_gather | solution.py:371
  532.8 12.0 fusion.139
  544.8 51.8 %all-gather.29.cloned.1.call-done = bf16[2048,1024]{1,0:T(8,128)(2,1)} async-done(((bf16[64,1024]{1,0:T(8,128)(2,1)}), bf16[2048,1024]{1,0:T(8,128)(2,1)}) %all-gather.29.cloned.1.call-update) | async-done | bytes 4194320 | tf_op jit(solution)/shard_map/all_gather | solution.py:372
  640.2 11.9 fusion.4
  694.5 15.9 fusion.19
  811.0 14.3 fusion.38
  884.1 40.9 %all-reduce.20 = (f32[1024]{0:T(1024)S(1)}, f32[4,1792]{1,0:T(4,128)S(1)}, f32[1792]{0:T(1024)S(1)}, f32[24]{0:T(128)}, f32[24]{0:T(128)}, /*index=5*/f32[24]{0:T(128)}, f32[1536]{0:T(1024)S(1)}, f32[1024]{0:T(1024)S(1)}) all-reduce(f32[1024]{0:T(1024)S(1)} %get-tuple-element.296, ...), channel_id=5, replica_groups=mesh['seq'=4,'dp'=8] {'seq','dp'}, use_global_device_ids=true, to_apply=%region_28.29.clone | all-reduce | flops 12616 | bytes 100928
  932.5 94.8 %reduce-scatter.24.cloned.1.call-done = f32[32,256]{1,0:T(8,128)} async-done(((f32[1024,256]{1,0:T(8,128)}), f32[32,256]{1,0:T(8,128)}) %reduce-scatter.24.cloned.1.call-update) | async-done | bytes 32784 | tf_op jit(solution)/shard_map/reduce_scatter | solution.py:535
  1027.4 136.2 %reduce-scatter.26.cloned.1.call-done = f32[16,1024]{1,0:T(8,128)} async-done(((f32[512,1024]{1,0:T(8,128)}), f32[16,1024]{1,0:T(8,128)}) %reduce-scatter.26.cloned.1.call-update) | async-done | bytes 65552 | tf_op jit(solution)/shard_map/reduce_scatter | solution.py:536
  1163.6 136.0 %reduce-scatter.22.cloned.1.call-done = f32[32,512]{1,0:T(8,128)} async-done(((f32[1024,512]{1,0:T(8,128)}), f32[32,512]{1,0:T(8,128)}) %reduce-scatter.22.cloned.1.call-update) | async-done | bytes 65552 | tf_op jit(solution)/shard_map/reduce_scatter | solution.py:534
  1299.6 117.7 %reduce-scatter.20.cloned.1.call-done = f32[48,1024]{1,0:T(8,128)} async-done(((f32[1536,1024]{1,0:T(8,128)}), f32[48,1024]{1,0:T(8,128)}) %reduce-scatter.20.cloned.1.call-update) | async-done | bytes 196624 | tf_op jit(solution)/shard_map/reduce_scatter | solution.py:533
  1417.4 119.9 %reduce-scatter.16.cloned.1.call-done = f32[32,1536]{1,0:T(8,128)} async-done(((f32[1024,1536]{1,0:T(8,128)}), f32[32,1536]{1,0:T(8,128)}) %reduce-scatter.16.cloned.1.call-update) | async-done | bytes 196624 | tf_op jit(solution)/shard_map/reduce_scatter | solution.py:527
  1537.3 154.0 %reduce-scatter.30.cloned.1.call-done = f32[64,1024]{1,0:T(8,128)} async-done(((f32[2048,1024]{1,0:T(8,128)}), f32[64,1024]{1,0:T(8,128)}) %reduce-scatter.30.cloned.1.call-update) | async-done | bytes 262160 | tf_op jit(solution)/shard_map/reduce_scatter | solution.py:430
  1691.2 150.4 %reduce-scatter.18.cloned.1.call-done = f32[32,1792]{1,0:T(8,128)} async-done(((f32[1024,1792]{1,0:T(8,128)}), f32[32,1792]{1,0:T(8,128)}) %reduce-scatter.18.cloned.1.call-update) | async-done | bytes 229392 | tf_op jit(solution)/shard_map/reduce_scatter | solution.py:528
  1841.6 187.2 %reduce-scatter.28.cloned.1.call-done = f32[32,4096]{1,0:T(8,128)} async-done(((f32[1024,4096]{1,0:T(8,128)}), f32[32,4096]{1,0:T(8,128)}) %reduce-scatter.28.cloned.1.call-update) | async-done | bytes 524304 | tf_op jit(solution)/shard_map/reduce_scatter | solution.py:429
  (493 shorter events, 398.0 us)
Async XLA Ops:
  7.2 177.4 %all-gather.15.cloned.1.call-start = ((), (), s32[]{:S(2)}) async-start(), calls=%async_computation.10 | async-start | bytes 3784704 | tf_op jit(solution)/shard_map/all_gather | solution.py:272
  7.9 214.7 %all-gather.21.cloned.1.call-start = ((), (), s32[]{:S(2)}) async-start(), calls=%async_computation.13 | async-start | bytes 1310720 | tf_op jit(solution)/shard_map/all_gather | solution.py:359
  103.3 122.4 %all-gather.23.cloned.1.call-start = ((), (), s32[]{:S(2)}) async-start(), calls=%async_computation.14 | async-start | bytes 1081344 | tf_op jit(solution)/shard_map/all_gather | solution.py:278
  104.0 170.9 %all-gather.31.cloned.1.call-start = ((), (), s32[]{:S(2)}) async-start(), calls=%async_computation.27 | async-start | bytes 7864320 | tf_op jit(solution)/shard_map/all_gather | solution.py:24
  184.6 492.5 %copy-start.53 = (f32[2,256,24]{1,2,0:T(8,128)}, f32[2,256,24]{1,2,0:T(8,128)S(1)}, u32[]{:S(2)}) copy-start(f32[2,256,24]{1,2,0:T(8,128)S(1)} %get-tuple-element.377) | copy-start | bytes 147460
  188.8 2.8 collective-permute-start
  203.6 133.3 %all-gather.17.cloned.1.call-start = ((), (), s32[]{:S(2)}) async-start(), calls=%async_computation.11 | async-start | bytes 3244032 | tf_op jit(solution)/shard_map/all_gather | solution.py:271
  204.2 193.6 %all-gather.19.cloned.1.call-start = ((), (), s32[]{:S(2)}) async-start(), calls=%async_computation.12 | async-start | bytes 3244032 | tf_op jit(solution)/shard_map/all_gather | solution.py:277
  204.8 248.6 %all-gather.25.cloned.1.call-start = ((), (), s32[]{:S(2)}) async-start(), calls=%async_computation.15 | async-start | bytes 1081344 | tf_op jit(solution)/shard_map/all_gather | solution.py:280
  205.6 327.3 %all-gather.27.cloned.1.call-start = ((), (), s32[]{:S(2)}) async-start(), calls=%async_computation.16 | async-start | bytes 8650752 | tf_op jit(solution)/shard_map/all_gather | solution.py:371
  206.3 390.3 %all-gather.29.cloned.1.call-start = ((), (), s32[]{:S(2)}) async-start(), calls=%async_computation.17 | async-start | bytes 4325376 | tf_op jit(solution)/shard_map/all_gather | solution.py:372
  207.0 509.2 %reduce-scatter.14.cloned.1.call-start = ((), (), s32[]{:S(2)}) async-start(), calls=%async_computation.18 | async-start | bytes 1310720 | tf_op jit(solution)/shard_map/reduce_scatter | solution.py:450
  210.8 482.6 %copy-start.88 = (f32[2,24,256]{2,1,0:T(8,128)}, f32[2,24,256]{2,1,0:T(8,128)S(1)}, u32[]{:S(2)}) copy-start(f32[2,24,256]{2,1,0:T(8,128)S(1)} %copy.302) | copy-start | bytes 147460
  656.9 72.4 %all-gather.33.cloned.1.call-start = ((), (), s32[]{:S(2)}) async-start(), calls=%async_computation.28 | async-start | bytes 3932160 | tf_op jit(solution)/shard_map/all_gather | solution.py:39
  681.4 249.7 %reduce-scatter.32.cloned.1.call-start = ((), (), s32[]{:S(2)}) async-start(), calls=%async_computation.29 | async-start | bytes 540672
  759.4 268.0 %reduce-scatter.24.cloned.1.call-start = ((), (), s32[]{:S(2)}) async-start(), calls=%async_computation.23 | async-start | bytes 1081344 | tf_op jit(solution)/shard_map/reduce_scatter | solution.py:535
  762.1 401.5 %reduce-scatter.26.cloned.1.call-start = ((), (), s32[]{:S(2)}) async-start(), calls=%async_computation.24 | async-start | bytes 2162688 | tf_op jit(solution)/shard_map/reduce_scatter | solution.py:536
  765.6 534.0 %reduce-scatter.22.cloned.1.call-start = ((), (), s32[]{:S(2)}) async-start(), calls=%async_computation.22 | async-start | bytes 2162688 | tf_op jit(solution)/shard_map/reduce_scatter | solution.py:534
  780.2 637.1 %reduce-scatter.20.cloned.1.call-start = ((), (), s32[]{:S(2)}) async-start(), calls=%async_computation.21 | async-start | bytes 6488064 | tf_op jit(solution)/shard_map/reduce_scatter | solution.py:533
  787.1 750.2 %reduce-scatter.16.cloned.1.call-start = ((), (), s32[]{:S(2)}) async-start(), calls=%async_computation.19 | async-start | bytes 6488064 | tf_op jit(solution)/shard_map/reduce_scatter | solution.py:527
  793.3 897.9 %reduce-scatter.30.cloned.1.call-start = ((), (), s32[]{:S(2)}) async-start(), calls=%async_computation.26 | async-start | bytes 8650752 | tf_op jit(solution)/shard_map/reduce_scatter | solution.py:430
  801.0 1040.6 %reduce-scatter.18.cloned.1.call-start = ((), (), s32[]{:S(2)}) async-start(), calls=%async_computation.20 | async-start | bytes 7569408 | tf_op jit(solution)/shard_map/reduce_scatter | solution.py:528
  844.3 5.9 collective-permute-start.1
  856.9 1171.9 %reduce-scatter.28.cloned.1.call-start = ((), (), s32[]{:S(2)}) async-start(), calls=%async_computation.25 | async-start | bytes 17301504 | tf_op jit(solution)/shard_map/reduce_scatter | solution.py:429
  (119 other events, 2887.0 us)
Sparse Core Ops, SparseCore 0:
  10.9 63.6 all-gather.14
  103.4 32.1 all-gather.20
  138.6 53.8 all-gather.22
  203.8 71.1 all-gather.30
  277.8 59.0 all-gather.16
  339.8 57.9 all-gather.18
  400.8 52.5 all-gather.24
  456.4 76.3 all-gather.26
  535.8 60.6 all-gather.28
  657.0 26.2 reduce-scatter.13
  685.3 43.9 all-gather.32
  759.5 133.9 reduce-scatter.31
  896.3 131.0 reduce-scatter.23
  1030.2 133.4 reduce-scatter.25
  1166.3 133.2 reduce-scatter.21
  1306.6 110.6 reduce-scatter.19
  1423.4 113.8 reduce-scatter.15
  1540.1 151.0 reduce-scatter.29
  1694.2 147.3 reduce-scatter.17
  1844.4 184.3 reduce-scatter.27
where the time goes:
time: 2040 us
  waiting for transfers between devices  1380 us (68%)
  matrix products  243 us (12%)
  blocking collectives  222 us (11%)
  other arithmetic  97.6 us (5%)
  local copies, waits for them, and re-layouts  72 us (4%)
    reduce_scatter x1, waiting for transfers between devices, local(): lax.psum_scatter(grad_gate_up_w, ('seq', 'dp'), scatter_dimension=0, tile...  187 us
    reduce_scatter x1, waiting for transfers between devices, local(): lax.psum_scatter(grad_down, ('seq', 'dp'), scatter_dimension=0, tiled=True)  154 us
    reduce_scatter x1, waiting for transfers between devices, local(): lax.psum_scatter(grad_input_w, ('seq', 'dp'), scatter_dimension=0, tiled=...  150 us
    reduce_scatter x1, waiting for transfers between devices, local(): lax.psum_scatter(grad_attn_w, ('seq', 'dp'), scatter_dimension=0, tiled=T...  136 us
    reduce_scatter x1, waiting for transfers between devices, local(): lax.psum_scatter(grad_query_w, ('seq', 'dp'), scatter_dimension=0, tiled=...  136 us
    reduce_scatter x1, waiting for transfers between devices, local(): lax.psum_scatter(grad_gate_w, ('seq', 'dp'), scatter_dimension=0, tiled=T...  120 us
    reduce_scatter x1, waiting for transfers between devices, local(): lax.psum_scatter(grad_mamba_out_w, ('seq', 'dp'), scatter_dimension=0, ti...  118 us
    reduce_scatter x1, waiting for transfers between devices, local(): lax.psum_scatter(grad_keyvalue_w, ('seq', 'dp'), scatter_dimension=0, til...  94.8 us
  transfers between devices with their start and end apart: 22, of which 17 were waited for; matrix products, arithmetic and copies ran while one was open for 15% of the time, Pallas kernels for 0%

commit v1 on v0

--- a/solution.py
+++ b/solution.py
@@ -10,7 +10,9 @@
 
 EPSILON = 1e-05
 THETA_BASE = 100000000000.0
-TOP_PRECISION = lax.Precision.HIGHEST
+TOP_PRECISION = lax.Precision.DEFAULT
+AXES = ("seq", "dp")
+LANES = 128
 
 
 def passed_along(block, axis, distance):
@@ -19,40 +21,31 @@
     return lax.ppermute(block, axis, route)
 
 
-def prefix(value, axis, join, neutral):
-    count, mine = (lax.axis_size(axis), lax.axis_index(axis))
-    pieces = jax.tree.map(lambda part: lax.all_gather(part, axis), value)
-    total = jax.tree.map(
-        lambda part, zero: jnp.full_like(part, 0) + jnp.asarray(zero, part.dtype), value, neutral
-    )
-
-    def prefix_step(position, total):
-        longer = join(total, jax.tree.map(lambda part: part[position], pieces))
-        return jax.tree.map(lambda new, old: jnp.where(position < mine, new, old), longer, total)
-
-    return lax.fori_loop(0, count - 1, prefix_step, total)
-
-
-def carried_in_2(x, axis, combine, identity):
-    peers, place = (lax.axis_size(axis), lax.axis_index(axis))
-    everything = jax.tree.map(
-        lambda part, kind: lax.all_gather(part.astype(kind), axis),
-        x,
-        jax.tree.map(lambda a: jnp.bfloat16 if a.dtype == jnp.float32 else a.dtype, x),
-    )
-    start = jax.tree.map(
-        lambda part, zero: jnp.broadcast_to(jnp.asarray(zero, part.dtype), part.shape), x, identity
-    )
-
-    def carried_step(k, before):
-        at = peers - 1 - k
-        reached = at > place
-        new = combine(
-            before, jax.tree.map(lambda part, own: part[at].astype(own.dtype), everything, x)
-        )
-        return jax.tree.map(lambda a, b: jnp.where(reached, a, b), new, before)
-
-    return lax.fori_loop(0, peers, carried_step, start)
+def pieces_of(decays, states):
+    seqs, heads, rows, cols = states.shape
+    high = decays.astype(jnp.bfloat16)
+    low = (decays - high.astype(jnp.float32)).astype(jnp.bfloat16)
+    pair = jnp.pad(jnp.stack([high, low], axis=1), ((0, 0), (0, 14), (0, cols - heads)))
+    packed = jnp.concatenate(
+        [states.astype(jnp.bfloat16).reshape(seqs, heads * rows, cols), pair], axis=1
+    )
+    everything = lax.all_gather(packed, "seq")
+    split = heads * rows
+    tail = everything[:, :, split : split + 2, :heads].astype(jnp.float32)
+    all_states = everything[:, :, :split].astype(jnp.float32)
+    return tail[:, :, 0] + tail[:, :, 1], all_states.reshape(-1, seqs, heads, rows, cols)
+
+
+def carried_states(decays, states, forward):
+    count, mine = (lax.axis_size("seq"), lax.axis_index("seq"))
+    all_decays, all_states = pieces_of(decays, states)
+    total = jnp.zeros_like(states)
+    order = range(count - 1) if forward else range(count - 1, 0, -1)
+    for at in order:
+        reached = at < mine if forward else at > mine
+        longer = all_decays[at][..., None, None] * total + all_states[at]
+        total = jnp.where(reached, longer, total)
+    return total
 
 
 def product(left_side, right_side):
@@ -80,10 +73,6 @@
     return inverse * grad_out - values * inverse**3 * jnp.mean(
         grad_out * values, axis=-1, keepdims=True
     )
-
-
-def chain_link(earlier, later_one):
-    return (earlier[0] * later_one[0], later_one[0][..., None, None] * earlier[1] + later_one[1])
 
 
 def rotate(values, places):
@@ -254,31 +243,55 @@
     seq_count, piece_len, model_width = hidden_in.shape
     seq_rank = lax.axis_index("seq")
     first_row = seq_rank * piece_len
-    (
-        gain_one,
-        gate_full,
-        input_full,
-        step_full,
-        taps_full,
-        bias_full,
-        gain_mamba,
-        output_full,
-        query_full,
-        keyvalue_full,
-        attn_full,
-    ) = (
-        lax.all_gather(mixer_gain, ("seq", "dp"), axis=0, tiled=True),
-        lax.all_gather(mamba_gate, ("seq", "dp"), axis=0, tiled=True),
-        lax.all_gather(mamba_input, ("seq", "dp"), axis=0, tiled=True),
-        lax.all_gather(step_weight, ("seq", "dp"), axis=0, tiled=True),
-        lax.all_gather(conv_taps, ("seq", "dp"), axis=1, tiled=True),
-        lax.all_gather(conv_bias, ("seq", "dp"), axis=0, tiled=True),
-        lax.all_gather(mamba_gain, ("seq", "dp"), axis=0, tiled=True),
-        lax.all_gather(mamba_output, ("seq", "dp"), axis=0, tiled=True),
-        lax.all_gather(query_weight, ("seq", "dp"), axis=0, tiled=True),
-        lax.all_gather(keyvalue_matrix, ("seq", "dp"), axis=0, tiled=True),
-        lax.all_gather(attn_output, ("seq", "dp"), axis=0, tiled=True),
-    )
+    devices = lax.axis_size(AXES)
+    rows_one = mamba_gate.shape[0]
+    width_gate, width_input = mamba_gate.shape[1], mamba_input.shape[1]
+    width_query, width_keyvalue = query_weight.shape[1], keyvalue_matrix.shape[1]
+    width_step = step_weight.shape[1]
+    small_parts = [mixer_gain, conv_taps.reshape(-1), conv_bias, mamba_gain, ffn_gain]
+    small = jnp.concatenate(small_parts)
+    width_small = -(-small.size // rows_one)
+    small = jnp.pad(small, (0, width_small * rows_one - small.size)).reshape(rows_one, width_small)
+    width_main = width_gate + width_input + width_query + width_keyvalue
+    rest = -(width_step + width_small) % LANES
+    first_pack = jnp.concatenate(
+        [
+            mamba_gate,
+            mamba_input,
+            query_weight,
+            keyvalue_matrix,
+            step_weight,
+            small,
+            jnp.zeros((rows_one, rest), small.dtype),
+        ],
+        axis=1,
+    )
+    second_pack = jnp.concatenate([mamba_output, attn_output], axis=0)
+    first_full = lax.all_gather(first_pack, AXES, axis=0, tiled=True)
+    first_full, second_pack, third_pack, fourth_pack = lax.optimization_barrier(
+        (first_full, second_pack, gate_up, down_weight)
+    )
+    second_full = lax.all_gather(second_pack, AXES, axis=0)
+    gate_up_full = lax.all_gather(third_pack, AXES, axis=0, tiled=True)
+    down_full = lax.all_gather(fourth_pack, AXES, axis=0, tiled=True)
+    main_full = first_full[:, :width_main]
+    step_full = first_full[:, width_main : width_main + width_step]
+    small_full = first_full[:, width_main + width_step : width_main + width_step + width_small]
+    small_full = small_full.reshape(devices, -1)
+    small_out = []
+    spot = 0
+    for part in small_parts:
+        small_out.append(small_full[:, spot : spot + part.size])
+        spot += part.size
+    gain_one = small_out[0].reshape(-1)
+    taps_full = small_out[1].reshape(devices, conv_taps.shape[0], -1)
+    taps_full = taps_full.transpose(1, 0, 2).reshape(conv_taps.shape[0], -1)
+    bias_full = small_out[2].reshape(-1)
+    gain_mamba = small_out[3].reshape(-1)
+    gain_two = small_out[4].reshape(-1)
+    rows_output = mamba_output.shape[0]
+    output_full = second_full[:, :rows_output].reshape(-1, mamba_output.shape[1])
+    attn_full = second_full[:, rows_output:].reshape(-1, attn_output.shape[1])
     rim_width = taps_full.shape[0] - 1
     doc_own = lax.dynamic_slice_in_dim(documents, first_row, piece_len, 1)
     doc_rim = lax.dynamic_slice_in_dim(
@@ -290,11 +303,13 @@
     inv_one = lax.rsqrt(jnp.mean(flat_rows * flat_rows, axis=-1, keepdims=True) + EPSILON)
     gain_first = gain_one.astype(jnp.float32)
     normed = (flat_rows * inv_one * gain_first).astype(jnp.bfloat16)
-    gate_pre = product(normed, gate_full)
-    conv_in = product(normed, input_full).astype(jnp.bfloat16)
+    main_raw = product(normed, main_full)
+    at_query = width_gate + width_input
+    gate_pre = main_raw[:, :width_gate]
+    conv_in = main_raw[:, width_gate:at_query].astype(jnp.bfloat16)
     step_raw = product(normed, step_full)
-    query_raw = product(normed, query_full)
-    keyvalue_raw = product(normed, keyvalue_full)
+    query_raw = main_raw[:, at_query : at_query + width_query]
+    keyvalue_raw = main_raw[:, at_query + width_query :]
     conv_width = conv_in.shape[1]
     conv_seq = conv_in.reshape(seq_count, piece_len, conv_width)
     rim_rows = passed_along(conv_seq[:, piece_len - rim_width :, :], "seq", 1)
@@ -330,9 +345,7 @@
         return jax.vmap(piece_carry)(xs_in, b_in, step_in, log_in, doc_own, prev_doc)
 
     (decays, states), carry_pull = jax.vjp(carry_fn, xs_all, b_all, step_seq, log_seq)
-    entered = prefix(
-        (decays, states), "seq", chain_link, (jnp.ones_like(decays), jnp.zeros_like(states))
-    )[1]
+    entered = carried_states(decays, states, True)
 
     def output_fn(xs_in, b_in, c_in, step_in, log_in, carried_in, skip_in):
         return jax.vmap(piece_output, in_axes=(0, 0, 0, 0, 0, 0, 0, 0, None))(
@@ -366,11 +379,6 @@
     attn_rows = attn_mix.reshape(seq_count * piece_len, -1).astype(jnp.bfloat16)
     attn_branch = product(attn_rows, attn_full)
     mixed_rows = flat_rows + mamba_branch + attn_branch
-    gain_two, gate_up_full, down_full = (
-        lax.all_gather(ffn_gain, ("seq", "dp"), axis=0, tiled=True),
-        lax.all_gather(gate_up, ("seq", "dp"), axis=0, tiled=True),
-        lax.all_gather(down_weight, ("seq", "dp"), axis=0, tiled=True),
-    )
     inv_two = lax.rsqrt(jnp.mean(mixed_rows * mixed_rows, axis=-1, keepdims=True) + EPSILON)
     gain_second = gain_two.astype(jnp.float32)
     normed_two = (mixed_rows * inv_two * gain_second).astype(jnp.bfloat16)
@@ -382,57 +390,29 @@
     ffn_act = (gate_silu * up_part).astype(jnp.bfloat16)
     ffn_branch = product(ffn_act, down_full)
     layer_out = (mixed_rows + ffn_branch).astype(jnp.bfloat16).reshape(hidden_in.shape)
-    (
-        gain_one,
-        gate_full,
-        input_full,
-        step_full,
-        taps_full,
-        bias_full,
-        gain_mamba,
-        output_full,
-        query_full,
-        keyvalue_full,
-        attn_full,
-        gain_two,
-        gate_up_full,
-        down_full,
-    ) = (
-        lax.all_gather(mixer_gain, ("seq", "dp"), axis=0, tiled=True),
-        lax.all_gather(mamba_gate, ("seq", "dp"), axis=0, tiled=True),
-        lax.all_gather(mamba_input, ("seq", "dp"), axis=0, tiled=True),
-        lax.all_gather(step_weight, ("seq", "dp"), axis=0, tiled=True),
-        lax.all_gather(conv_taps, ("seq", "dp"), axis=1, tiled=True),
-        lax.all_gather(conv_bias, ("seq", "dp"), axis=0, tiled=True),
-        lax.all_gather(mamba_gain, ("seq", "dp"), axis=0, tiled=True),
-        lax.all_gather(mamba_output, ("seq", "dp"), axis=0, tiled=True),
-        lax.all_gather(query_weight, ("seq", "dp"), axis=0, tiled=True),
-        lax.all_gather(keyvalue_matrix, ("seq", "dp"), axis=0, tiled=True),
-        lax.all_gather(attn_output, ("seq", "dp"), axis=0, tiled=True),
-        lax.all_gather(ffn_gain, ("seq", "dp"), axis=0, tiled=True),
-        lax.all_gather(gate_up, ("seq", "dp"), axis=0, tiled=True),
-        lax.all_gather(down_weight, ("seq", "dp"), axis=0, tiled=True),
-    )
     grad_out = cotangent.reshape(-1, model_width).astype(jnp.float32)
     grad_ffn_branch = grad_out.astype(jnp.bfloat16)
-    grad_down = product_tn(ffn_act, grad_ffn_branch)
+    grad_down = product_tn(ffn_act, grad_ffn_branch).astype(jnp.bfloat16)
     grad_act = product_nt(grad_ffn_branch, down_full)
     grad_gate_up_rows = jnp.concatenate(
         [grad_act * up_part * silu_slope(gate_part), grad_act * gate_silu], axis=1
     ).astype(jnp.bfloat16)
-    grad_gate_up_w = product_tn(normed_two, grad_gate_up_rows)
+    grad_pieces = [
+        product_tn(normed_two, grad_gate_up_rows[:, at : at + model_width]).astype(jnp.bfloat16)
+        for at in range(0, grad_gate_up_rows.shape[1], model_width)
+    ]
     grad_normed_two = product_nt(grad_gate_up_rows, gate_up_full)
     grad_gain_two = jnp.sum(grad_normed_two * mixed_rows * inv_two, axis=0)
     mixed_gradient = grad_out + norm_back(mixed_rows, inv_two, grad_normed_two * gain_second)
-    grad_gain_two, grad_gate_up_w, grad_down = (
-        lax.psum_scatter(grad_gain_two, ("seq", "dp"), scatter_dimension=0, tiled=True),
-        lax.psum_scatter(grad_gate_up_w, ("seq", "dp"), scatter_dimension=0, tiled=True),
-        lax.psum_scatter(grad_down, ("seq", "dp"), scatter_dimension=0, tiled=True),
-    )
+    ffn_pack = jnp.concatenate(
+        [part.reshape(devices, -1, model_width) for part in (*grad_pieces, grad_down)], axis=1
+    )
+    ffn_pack, mixed_gradient = lax.optimization_barrier((ffn_pack, mixed_gradient))
+    ffn_sums = lax.psum_scatter(ffn_pack, AXES, scatter_dimension=0)
     grad_branch = mixed_gradient.astype(jnp.bfloat16)
-    grad_attn_w = product_tn(attn_rows, grad_branch)
+    grad_attn_w = product_tn(attn_rows, grad_branch).astype(jnp.bfloat16)
     grad_attn_rows = product_nt(grad_branch, attn_full).astype(jnp.bfloat16)
-    grad_mamba_out_w = product_tn(mamba_norm, grad_branch)
+    grad_mamba_out_w = product_tn(mamba_norm, grad_branch).astype(jnp.bfloat16)
     grad_mamba_norm = product_nt(grad_branch, output_full)
     grad_gain_mamba = jnp.sum(grad_mamba_norm * gated_rows * inv_mamba, axis=0)
     grad_gated = norm_back(gated_rows, inv_mamba, grad_mamba_norm * gain_mamba.astype(jnp.float32))
@@ -461,12 +441,7 @@
     grad_xs_one, grad_b_one, grad_c_one, grad_step_one, grad_log_one, grad_entered, grad_skip = (
         output_pull(grad_ssm.reshape(ssm_out.shape))
     )
-    leaving = carried_in_2(
-        (decays, grad_entered),
-        "seq",
-        chain_link,
-        (jnp.ones_like(decays), jnp.zeros_like(grad_entered)),
-    )[1]
+    leaving = carried_states(decays, grad_entered, False)
     grad_decays = jnp.sum(leaving * entered, axis=(2, 3))
     grad_xs_two, grad_b_two, grad_step_two, grad_log_two = carry_pull((grad_decays, leaving))
     grad_log = (grad_log_one + grad_log_two).reshape(-1, heads_ssm)
@@ -492,52 +467,75 @@
         [jnp.zeros((seq_count, piece_len - rim_width, conv_width), jnp.float32), rim_grads], axis=1
     )
     grad_conv_in = grad_conv_in.reshape(-1, conv_width).astype(jnp.bfloat16)
-    grad_normed = (
-        product_nt(grad_gate_pre, gate_full)
-        + product_nt(grad_conv_in, input_full)
-        + product_nt(grad_step_raw, step_full)
-        + product_nt(grad_query_raw, query_full)
-        + product_nt(grad_keyvalue_raw, keyvalue_full)
-    )
-    grad_gate_w = product_tn(normed, grad_gate_pre)
-    grad_input_w = product_tn(normed, grad_conv_in)
-    grad_step_w = product_tn(normed, grad_step_raw)
-    grad_query_w = product_tn(normed, grad_query_raw)
-    grad_keyvalue_w = product_tn(normed, grad_keyvalue_raw)
+    grad_main = jnp.concatenate(
+        [grad_gate_pre, grad_conv_in, grad_query_raw, grad_keyvalue_raw], axis=1
+    )
+    grad_normed = product_nt(grad_main, main_full) + product_nt(grad_step_raw, step_full)
+    main_pieces = [
+        product_tn(normed, grad_main[:, at : at + model_width]).astype(jnp.bfloat16)
+        for at in range(0, width_main, model_width)
+    ]
+    grad_step_w = product_tn(normed, grad_step_raw).astype(jnp.bfloat16)
     grad_gain_one = jnp.sum(grad_normed * flat_rows * inv_one, axis=0)
     grad_input = (
         (mixed_gradient + norm_back(flat_rows, inv_one, grad_normed * gain_first))
         .astype(jnp.bfloat16)
         .reshape(hidden_in.shape)
     )
-    (
-        grad_gain_one,
-        grad_gate_w,
-        grad_input_w,
-        grad_step_w,
-        grad_taps,
-        grad_conv_b,
-        grad_gain_mamba,
-        grad_mamba_out_w,
-        grad_query_w,
-        grad_keyvalue_w,
-        grad_attn_w,
-    ) = (
-        lax.psum_scatter(grad_gain_one, ("seq", "dp"), scatter_dimension=0, tiled=True),
-        lax.psum_scatter(grad_gate_w, ("seq", "dp"), scatter_dimension=0, tiled=True),
-        lax.psum_scatter(grad_input_w, ("seq", "dp"), scatter_dimension=0, tiled=True),
-        lax.psum_scatter(grad_step_w, ("seq", "dp"), scatter_dimension=0, tiled=True),
-        lax.psum_scatter(grad_taps, ("seq", "dp"), scatter_dimension=1, tiled=True),
-        lax.psum_scatter(grad_conv_b, ("seq", "dp"), scatter_dimension=0, tiled=True),
-        lax.psum_scatter(grad_gain_mamba, ("seq", "dp"), scatter_dimension=0, tiled=True),
-        lax.psum_scatter(grad_mamba_out_w, ("seq", "dp"), scatter_dimension=0, tiled=True),
-        lax.psum_scatter(grad_query_w, ("seq", "dp"), scatter_dimension=0, tiled=True),
-        lax.psum_scatter(grad_keyvalue_w, ("seq", "dp"), scatter_dimension=0, tiled=True),
-        lax.psum_scatter(grad_attn_w, ("seq", "dp"), scatter_dimension=0, tiled=True),
-    )
-    grad_step_bias, grad_decay_log, grad_skip = lax.psum(
-        (grad_step_bias, grad_decay_log, grad_skip), ("seq", "dp")
-    )
+    taps_count = conv_taps.shape[0]
+    grad_taps = grad_taps.reshape(taps_count, devices, -1).transpose(1, 0, 2)
+    small_grads = jnp.concatenate(
+        [
+            part.reshape(devices, -1)
+            for part in (grad_gain_one, grad_taps, grad_conv_b, grad_gain_mamba, grad_gain_two)
+        ],
+        axis=1,
+    ).astype(jnp.bfloat16)
+    small_rows = [
+        jnp.pad(part, ((0, 0), (0, model_width - part.shape[1])))[:, None, :]
+        for part in (grad_step_w.reshape(devices, -1), small_grads)
+    ]
+    mixer_parts = [
+        part.reshape(devices, -1, model_width)
+        for part in (*main_pieces, grad_mamba_out_w, grad_attn_w)
+    ]
+    spare = jnp.zeros((devices, 14, model_width), jnp.bfloat16)
+    mixer_pack = jnp.concatenate([*mixer_parts, *small_rows, spare], axis=1)
+    head_grads = jnp.stack([grad_step_bias, grad_decay_log, grad_skip])
+    head_sums = jnp.sum(lax.all_gather(head_grads, AXES), axis=0)
+    grad_step_bias, grad_decay_log, grad_skip = head_sums[0], head_sums[1], head_sums[2]
+    mixer_pack, ffn_sums = lax.optimization_barrier((mixer_pack, ffn_sums))
+    mixer_sums = lax.psum_scatter(mixer_pack, AXES, scatter_dimension=0).astype(jnp.float32)
+    ffn_sums = ffn_sums.astype(jnp.float32)
+
+    def widened(rows, count):
+        return jnp.concatenate([rows[i * rows_one : (i + 1) * rows_one] for i in range(count)], 1)
+
+    ffn_count = len(grad_pieces)
+    grad_gate_up_w = widened(ffn_sums, ffn_count)
+    grad_down = ffn_sums[ffn_count * rows_one :]
+    main_count = len(main_pieces)
+    main_sums = widened(mixer_sums, main_count)
+    grad_gate_w = main_sums[:, :width_gate]
+    grad_input_w = main_sums[:, width_gate:at_query]
+    grad_query_w = main_sums[:, at_query : at_query + width_query]
+    grad_keyvalue_w = main_sums[:, at_query + width_query :]
+    at_row = main_count * rows_one
+    grad_mamba_out_w = mixer_sums[at_row : at_row + rows_output]
+    at_row += rows_output
+    grad_attn_w = mixer_sums[at_row : at_row + attn_output.shape[0]]
+    at_row += attn_output.shape[0]
+    grad_step_w = mixer_sums[at_row, : step_weight.size].reshape(step_weight.shape)
+    small_out = []
+    spot = 0
+    for part in small_parts:
+        small_out.append(mixer_sums[at_row + 1, spot : spot + part.size])
+        spot += part.size
+    grad_gain_one = small_out[0]
+    grad_taps = small_out[1].reshape(taps_count, -1)
+    grad_conv_b = small_out[2]
+    grad_gain_mamba = small_out[3]
+    grad_gain_two = small_out[4]
     return (
         layer_out,
         grad_input,

time: 2040 us -> 948 us (0.46)
  waiting for transfers between devices: 1380 us -> 362 us
  blocking collectives: 222 us -> 39.1 us
  local copies, waits for them, and re-layouts: 72 us -> 203 us
  matrix products: 243 us -> 180 us
  other arithmetic: 97.6 us -> 129 us
    reduce_scatter x8 -> x2, waiting for transfers between devices: 1100 us -> 115 us  [the longest x1 115 us: local(): lax.psum_scatter(mixer_pack, AXES, scatter_dimension=0).astype(jnp.float32)]
    all_gather x5 -> x1, blocking collectives: 138 us -> 39.1 us  [local(): head_sums = jnp.sum(lax.all_gather(head_grads, AXES), axis=0)]
    unnamed x2 -> x0, blocking collectives: 83.1 us -> none
    concatenate x0 -> x6, local copies, waits for them, and re-layouts: none -> 78 us  [the longest x1 70.9 us: local(): mixer_pack = jnp.concatenate([*mixer_parts, *small_rows, spare], axis=1)]
    all_gather x9 -> x6, waiting for transfers between devices: 274 us -> 242 us  [the longest x1 73.2 us: local(): first_full = lax.all_gather(first_pack, AXES, axis=0, tiled=True)]
    slice x3 -> x21, local copies, waits for them, and re-layouts: 0.54 us -> 21 us  [the longest x2 4.81 us: local(): query_raw = main_raw[:, at_query:at_query + width_query]]
    dot_general x8 -> x12, matrix products: 44.2 us -> 28 us  [product_tn(): lax.dot_general(left_side, right_side, (((0,), (0,)), ((), ())), preferre...]
    dot_general x9 -> x6, matrix products: 41.5 us -> 33.6 us  [product(): return jnp.dot(left_side, right_side, preferred_element_type=jnp.float32)]
  transfers between devices with their start and end apart: 22 -> 12, of which waited for: 17 -> 7; matrix products, arithmetic and copies ran while one was open for 15% -> 41% of each run, Pallas kernels for 0% -> 0%
where the time goes in v1:
time: 948 us; the launch traced here: 934 us
  waiting for transfers between devices  362 us (38%)
  local copies, waits for them, and re-layouts  203 us (21%)
  matrix products  180 us (19%)
  other arithmetic  129 us (14%)
  blocking collectives  39.1 us (4%)
  between operations  16.8 us (2%)
    reduce_scatter x1, waiting for transfers between devices, local(): lax.psum_scatter(mixer_pack, AXES, scatter_dimension=0).astype(jnp.float32)  115 us
    all_gather x1, waiting for transfers between devices, local(): first_full = lax.all_gather(first_pack, AXES, axis=0, tiled=True)  73.2 us
    concatenate x1, local copies, waits for them, and re-layouts, local(): mixer_pack = jnp.concatenate([*mixer_parts, *small_rows, spare], axis=1)  70.9 us
    all_gather x1, waiting for transfers between devices, local(): gate_up_full = lax.all_gather(third_pack, AXES, axis=0, tiled=True)  69.8 us
    all_gather x1, waiting for transfers between devices, local(): down_full = lax.all_gather(fourth_pack, AXES, axis=0, tiled=True)  52.1 us
    all_gather x1, blocking collectives, local(): head_sums = jnp.sum(lax.all_gather(head_grads, AXES), axis=0)  39.1 us
    dot_general x6, matrix products, product_nt(): lax.dot_general(left_side, right_side, (((1,), (1,)), ((), ())), preferre...  34.2 us
    dot_general x6, matrix products, product(): return jnp.dot(left_side, right_side, preferred_element_type=jnp.float32)  33.6 us
  transfers between devices with their start and end apart: 12, of which 7 were waited for; matrix products, arithmetic and copies ran while one was open for 41% of the time, Pallas kernels for 0%

profile of v1, /device:TPU:0, one launch (start us, length us, event | category | flops | bytes accessed | tf_op | source)
XLA Modules:
  0.0 934.0 jit_solution(12795237587106058214)
XLA Ops:
  21.5 73.2 %all-gather.13.cloned.1.call-done = bf16[1024,4224]{1,0:T(8,128)(2,1)} async-done(((bf16[32,4224]{1,0:T(8,128)(2,1)}), bf16[1024,4224]{1,0:T(8,128)(2,1)}) %all-gather.13.cloned.1.call-update) | async-done | bytes 8650768 | tf_op jit(solution)/shard_map/all_gather | solution.py:270
  97.4 10.5 %fusion.165 = (bf16[512,4096]{1,0:T(8,128)(2,1)S(1)}, f32[512,4096]{1,0:T(8,128)}) fusion(bf16[512,1024]{1,0:T(8,128)(2,1)S(1)} %fusion.61, bf16[1024,4224]{1,0:T(8,128)(2,1)} %all-gather.13.cloned.1.call-done), kind=kOutput, calls=%fused_computation.359 | convolution fusion | flops 4297064448 | bytes 22020096 | tf_op jit(solution)/shard_map/dot_general | solution.py:52
  162.4 7.3 fusion.166
  169.7 8.0 fusion.3
  177.7 7.9 fusion.95
  187.0 13.5 %all-gather.21.cloned.1.call-done = bf16[8,1552,128]{2,1,0:T(8,128)(2,1)} async-done(((bf16[2,1552,128]{2,1,0:T(8,128)(2,1)}), bf16[8,1552,128]{2,1,0:T(8,128)(2,1)}) %all-gather.21.cloned.1.call-update) | async-done | bytes 3178512 | tf_op jit(solution)/shard_map/all_gather | solution.py:32
  222.7 6.6 reshape.787
  233.2 32.9 %all-gather.23.cloned.1.call-done = bf16[2048,1024]{1,0:T(8,128)(2,1)} async-done(((bf16[64,1024]{1,0:T(8,128)(2,1)}), bf16[2048,1024]{1,0:T(8,128)(2,1)}) %all-gather.23.cloned.1.call-update) | async-done | bytes 4194320 | tf_op jit(solution)/shard_map/all_gather | solution.py:274
  275.1 69.8 %all-gather.17.cloned.1.call-done = bf16[1024,4096]{1,0:T(8,128)(2,1)} async-done(((bf16[32,4096]{1,0:T(8,128)(2,1)}), bf16[1024,4096]{1,0:T(8,128)(2,1)}) %all-gather.17.cloned.1.call-update) | async-done | bytes 8388624 | tf_op jit(solution)/shard_map/all_gather | solution.py:275
  344.9 11.5 %fusion.167 = f32[512,4096]{1,0:T(8,128)} fusion(bf16[512,1024]{1,0:T(8,128)(2,1)} %multiply_convert_fusion.4, bf16[1024,4096]{1,0:T(8,128)(2,1)} %all-gather.17.cloned.1.call-done), kind=kOutput, calls=%fused_computation.361 | convolution fusion | flops 4294967296 | bytes 17825792 | tf_op jit(solution)/shard_map/dot_general | solution.py:52
  356.4 52.1 %all-gather.19.cloned.1.call-done = bf16[2048,1024]{1,0:T(8,128)(2,1)} async-done(((bf16[64,1024]{1,0:T(8,128)(2,1)}), bf16[2048,1024]{1,0:T(8,128)(2,1)}) %all-gather.19.cloned.1.call-update) | async-done | bytes 4194320 | tf_op jit(solution)/shard_map/all_gather | solution.py:276
  408.5 8.5 fusion.40
  422.3 10.0 %multiply_reduce_fusion.10 = (bf16[1024]{0:T(1024)(128)(2,1)S(1)}, f32[512]{0:T(512)S(1)}, f32[512,1024]{1,0:T(8,128)}) fusion(f32[512,1024]{1,0:T(8,128)S(1)} %get-tuple-element.283, f32[512]{0:T(512)S(1)} %get-tuple-element.273, f32[1024]{0:T(1024)S(1)} %reshape.765, bf16[1024,4096]{1,0:T(8,128)(2,1)} %all-gather.17.cloned.1.call-done, ...), kind=kOutput, calls=%fused_computation.120 | convolution fusion | flops 4306500096 | bytes 16787456 | tf_op jit(solution)/shard_map/dot_general | solution.py:62
  452.3 9.4 %fusion.90 = bf16[2,2,64,1024]{3,2,1,0:T(8,128)(2,1)} fusion(bf16[2,256,2,4,64]{1,4,3,2,0:T(8,128)(2,1)S(1)} %copy.516, f32[2,2,4,256,1024]{3,4,2,1,0:T(8,128)} %get-tuple-element.281, f32[2,2,4,256]{3,2,1,0:T(4,128)S(1)} %bitcast.401), kind=kOutput, calls=%fused_computation.154 | convolution fusion | flops 545521664 | bytes 17842176 | tf_op jit(solution)/shard_map/vmap(ncuy,uncp->ynp)/dot_general | solution.py:205
  461.8 13.0 %fusion = (f32[2,2,4,256]{3,2,1,0:T(4,128)S(1)}, f32[2,2,1024,256,4]{3,2,4,1,0:T(8,128)}) fusion(f32[2,2,4,256,1024]{3,4,2,1,0:T(8,128)} %get-tuple-element.281, f32[2,2,4,256]{3,2,1,0:T(4,128)S(1)} %bitcast.402, bf16[2,1024,2,64,1]{1,3,4,2,0:T(8,128)(2,1)S(1)} %bitcast.370, bf16[2,256,2,4,64]{1,4,3,2,0:T(8,128)(2,1)S(1)} %copy.516), kind=kOutput, calls=%fused_computation.2 | convolution fusion | flops 549449728 | bytes 34635776 | tf_op jit(solution)/shard_map/vmap(lbon,ybn->boly)/dot_general | solution.py:194
  475.1 7.9 fusion.2
  516.2 11.4 %fusion.21 = (f32[2,24,256]{2,1,0:T(8,128)}, f32[2,24,256]{2,1,0:T(8,128)}, f32[2,24,256]{2,1,0:T(8,128)}, bf16[2,256,256]{2,1,0:T(8,128)(2,1)}) fusion(f32[2,24,256]{2,1,0:T(8,128)} %copy.481, f32[2,256,256]{2,1,0:T(8,128)} %fusion.125, f32[2,24,256]{2,1,0:T(8,128)S(1)} %copy-done.69, pred[2,256,256]{2,1,0:T(8,128)(4,1)} %compare_and_fusion.1, ...), kind=kOutput, calls=%fused_computation.28 | convolution fusion | flops 449671168 | bytes 5881856 | tf_op jit(solution)/shard_map/transpose(jvp(vmap(hts,shp->thp)))/dot_general | solution.py:132
  563.4 6.8 constant_dynamic-update-slice_fusion.9
  594.3 9.6 %multiply_reduce_fusion.13 = (f32[2,1536]{1,0:T(2,128)}, f32[1,2,1536,128]{3,2,1,0:T(8,128)}) fusion(f32[2,1536]{1,0:T(2,128)S(1)} %copy-done.89, f32[2,1536]{1,0:T(2,128)S(1)} %copy-done.91, f32[2,1536]{1,0:T(2,128)S(1)} %copy-done.90, f32[2,1536]{1,0:T(2,128)S(1)} %mul.898, f32[2,1536]{1,0:T(2,128)S(1)} %copy-done.93, f32[2,1536]{1,0:T(2,128)S(1)} %copy-done.92, ...), kind=kLoop, calls=%fused_computation.138 | loop fusion | flops 7074816 | bytes 11096070 | tf_op jit(solution)/shard_map/reduce_sum | solution.py:445
  659.8 7.2 fusion.16
  679.9 70.9 %concatenate.119 = bf16[32,208,1024]{2,1,0:T(8,128)(2,1)} concatenate(bf16[32,32,1024]{2,1,0:T(8,128)(2,1)} %bitcast.381, bf16[32,32,1024]{2,1,0:T(8,128)(2,1)} %bitcast.382, bf16[32,32,1024]{2,1,0:T(8,128)(2,1)} %bitcast.383, bf16[32,32,1024]{2,1,0:T(8,128)(2,1)} %bitcast.384, bf16[32,48,1024]{2,1,0:T(8,128)(2,1)} %bitcast.364, bf16[32,16,1024]{2,1,0:T(8,128)(2,1)} %bitcast.394, ...), dimensions={1} | concatenate | bytes 27262976 | tf_op jit(solution)/shard_map/concatenate | solution.py:503
  751.7 6.9 add_convert_fusion
  758.7 39.1 %all-gather.4 = f32[32,3,24]{2,1,0:T(4,128)S(1)} all-gather(f32[1,3,24]{2,1,0:T(4,128)S(1)} %maximum_bitcast_fusion), channel_id=5, replica_groups=mesh['seq'=4,'dp'=8] {'seq','dp'}, dimensions={0}, use_global_device_ids=true | all-gather | bytes 9504 | tf_op jit(solution)/shard_map/all_gather | solution.py:505
  803.2 115.2 %reduce-scatter.8.cloned.1.call-done = bf16[1,208,1024]{2,1,0:T(8,128)(2,1)} async-done(((bf16[32,208,1024]{2,1,0:T(8,128)(2,1)}), bf16[1,208,1024]{2,1,0:T(8,128)(2,1)}) %reduce-scatter.8.cloned.1.call-update) | async-done | bytes 426000 | tf_op jit(solution)/shard_map/reduce_scatter | solution.py:508
  (559 shorter events, 307.9 us)
Async XLA Ops:
  7.2 87.6 %all-gather.13.cloned.1.call-start = ((), (), s32[]{:S(2)}) async-start(), calls=%async_computation.3 | async-start | bytes 8921088 | tf_op jit(solution)/shard_map/all_gather | solution.py:270
  13.5 146.6 %all-gather.15.cloned.1.call-start = ((), (), s32[]{:S(2)}) async-start(), calls=%async_computation.4 | async-start | bytes 1310720 | tf_op jit(solution)/shard_map/all_gather | solution.py:372
  14.2 95.5 %copy-start.121 = (f32[24]{0:T(128)}, f32[24]{0:T(128)S(1)}, u32[]{:S(2)}) copy-start(f32[24]{0:T(128)S(1)} %exp.63) | copy-start | bytes 292
  15.8 92.1 %copy-start.87 = (f32[1,2,2,128]{3,1,2,0:T(2,128)}, f32[1,2,2,128]{3,1,2,0:T(2,128)S(1)}, u32[]{:S(2)}) copy-start(f32[1,2,2,128]{3,1,2,0:T(2,128)S(1)} %copy.629) | copy-start | bytes 6148
  17.5 95.9 %copy-start.123 = (pred[2]{0:T(512)(128)(4,1)}, pred[2]{0:T(512)(128)(4,1)S(1)}, u32[]{:S(2)}) copy-start(pred[2]{0:T(512)(128)(4,1)S(1)} %eq.85) | copy-start | bytes 10
  18.3 106.1 %copy-start.105 = (pred[2,256]{1,0:T(4,128)(4,1)}, pred[2,256]{1,0:T(4,128)(4,1)S(1)}, u32[]{:S(2)}) copy-start(pred[2,256]{1,0:T(4,128)(4,1)S(1)} %get-tuple-element.260) | copy-start | bytes 1540
  18.4 106.1 %copy-start.107 = (pred[2,256]{1,0:T(4,128)(4,1)}, pred[2,256]{1,0:T(4,128)(4,1)S(1)}, u32[]{:S(2)}) copy-start(pred[2,256]{1,0:T(4,128)(4,1)S(1)} %get-tuple-element.261) | copy-start | bytes 1540
  18.4 106.1 %copy-start.109 = (pred[2,256]{1,0:T(4,128)(4,1)}, pred[2,256]{1,0:T(4,128)(4,1)S(1)}, u32[]{:S(2)}) copy-start(pred[2,256]{1,0:T(4,128)(4,1)S(1)} %get-tuple-element.262) | copy-start | bytes 1540
  18.6 102.2 %copy-start.65 = (pred[2,256]{0,1:T(8,128)(4,1)}, pred[2,256]{0,1:T(8,128)(4,1)S(1)}, u32[]{:S(2)}) copy-start(pred[2,256]{0,1:T(8,128)(4,1)S(1)} %copy.485) | copy-start | bytes 1540
  115.0 9.0 collective-permute-start
  120.7 79.8 %all-gather.21.cloned.1.call-start = ((), (), s32[]{:S(2)}) async-start(), calls=%async_computation.10 | async-start | bytes 3973120 | tf_op jit(solution)/shard_map/all_gather | solution.py:32
  136.0 130.1 %all-gather.23.cloned.1.call-start = ((), (), s32[]{:S(2)}) async-start(), calls=%async_computation.11 | async-start | bytes 4325376 | tf_op jit(solution)/shard_map/all_gather | solution.py:274
  136.6 208.3 %all-gather.17.cloned.1.call-start = ((), (), s32[]{:S(2)}) async-start(), calls=%async_computation.5 | async-start | bytes 8650752 | tf_op jit(solution)/shard_map/all_gather | solution.py:275
  137.2 271.3 %all-gather.19.cloned.1.call-start = ((), (), s32[]{:S(2)}) async-start(), calls=%async_computation.6 | async-start | bytes 4325376 | tf_op jit(solution)/shard_map/all_gather | solution.py:276
  144.7 348.4 %copy-start.81 = (f32[1536]{0:T(1024)}, f32[1536]{0:T(1024)S(1)}, u32[]{:S(2)}) copy-start(f32[1536]{0:T(1024)S(1)} %reshape.764) | copy-start | bytes 18436
  155.3 422.0 %reduce-scatter.4.cloned.1.call-start = ((), (), s32[]{:S(2)}) async-start(), calls=%async_computation.7 | async-start | bytes 1310720 | tf_op jit(solution)/shard_map/reduce_scatter | solution.py:430
  233.2 259.9 %copy-start.100 = (f32[512]{0:T(512)}, f32[512]{0:T(512)S(1)}, u32[]{:S(2)}) copy-start(f32[512]{0:T(512)S(1)} %get-tuple-element.271) | copy-start | bytes 6148
  233.2 259.9 %copy-start.102 = (f32[512]{0:T(512)}, f32[512]{0:T(512)S(1)}, u32[]{:S(2)}) copy-start(f32[512]{0:T(512)S(1)} %get-tuple-element.270) | copy-start | bytes 6148
  273.6 171.5 %copy-start.15 = (f32[512,1024]{1,0:T(8,128)}, f32[512,1024]{1,0:T(8,128)S(1)}, u32[]{:S(2)}) copy-start(f32[512,1024]{1,0:T(8,128)S(1)} %get-tuple-element.283) | copy-start | bytes 6291460
  275.1 133.4 %copy-start.50 = (bf16[2,256,1024]{2,1,0:T(8,128)(2,1)S(1)}, bf16[2,256,1024]{2,1,0:T(8,128)(2,1)}, u32[]{:S(2)}) copy-start(bf16[2,256,1024]{2,1,0:T(8,128)(2,1)} %param.22) | copy-start | bytes 3145732
  487.4 96.0 %all-gather.25.cloned.1.call-start = ((), (), s32[]{:S(2)}) async-start(), calls=%async_computation.12 | async-start | bytes 3973120 | tf_op jit(solution)/shard_map/all_gather | solution.py:32
  509.0 241.8 %reduce-scatter.6.cloned.1.call-start = ((), (), s32[]{:S(2)}) async-start(), calls=%async_computation.8 | async-start | bytes 12976128 | tf_op jit(solution)/shard_map/reduce_scatter | solution.py:411
  553.9 364.4 %reduce-scatter.8.cloned.1.call-start = ((), (), s32[]{:S(2)}) async-start(), calls=%async_computation.9 | async-start | bytes 14057472 | tf_op jit(solution)/shard_map/reduce_scatter | solution.py:508
  649.6 6.0 collective-permute-start.1
  (120 other events, 1043.0 us)
Sparse Core Ops, SparseCore 0:
  13.6 81.0 all-gather.12
  120.8 33.4 all-gather.14
  156.2 44.2 all-gather.20
  203.9 62.1 all-gather.22
  268.9 75.9 all-gather.16
  347.8 60.6 all-gather.18
  487.5 26.2 reduce-scatter.3
  515.8 44.2 all-gather.24
  567.2 155.5 reduce-scatter.5
  751.0 167.2 reduce-scatter.7

commit v2 on v1

--- a/solution.py
+++ b/solution.py
@@ -16,35 +16,29 @@
 
 
 def passed_along(block, axis, distance):
+    if lax.axis_size(axis) == 1:
+        return jnp.zeros_like(block)
     devices = range(lax.axis_size(axis))
     route = [(i - distance, i) for i in devices if i - distance in devices]
     return lax.ppermute(block, axis, route)
 
 
-def pieces_of(decays, states):
+def carried_states(decays, states, direction):
     seqs, heads, rows, cols = states.shape
     high = decays.astype(jnp.bfloat16)
     low = (decays - high.astype(jnp.float32)).astype(jnp.bfloat16)
     pair = jnp.pad(jnp.stack([high, low], axis=1), ((0, 0), (0, 14), (0, cols - heads)))
+    split = heads * rows
     packed = jnp.concatenate(
-        [states.astype(jnp.bfloat16).reshape(seqs, heads * rows, cols), pair], axis=1
-    )
-    everything = lax.all_gather(packed, "seq")
-    split = heads * rows
-    tail = everything[:, :, split : split + 2, :heads].astype(jnp.float32)
-    all_states = everything[:, :, :split].astype(jnp.float32)
-    return tail[:, :, 0] + tail[:, :, 1], all_states.reshape(-1, seqs, heads, rows, cols)
-
-
-def carried_states(decays, states, forward):
-    count, mine = (lax.axis_size("seq"), lax.axis_index("seq"))
-    all_decays, all_states = pieces_of(decays, states)
-    total = jnp.zeros_like(states)
-    order = range(count - 1) if forward else range(count - 1, 0, -1)
-    for at in order:
-        reached = at < mine if forward else at > mine
-        longer = all_decays[at][..., None, None] * total + all_states[at]
-        total = jnp.where(reached, longer, total)
+        [states.astype(jnp.bfloat16).reshape(seqs, split, cols), pair], axis=1
+    )
+    total, passed = 0.0, 1.0
+    for distance in range(1, lax.axis_size("seq")):
+        arrived = passed_along(packed, "seq", direction * distance).astype(jnp.float32)
+        tail = arrived[:, split] + arrived[:, split + 1]
+        far_states = arrived[:, :split].reshape(states.shape)
+        total = total + passed * far_states
+        passed = passed * tail[:, :heads, None, None]
     return total
 
 
@@ -106,8 +100,13 @@
     return summed
 
 
-def piece_carry(xs_piece, b_piece, step_piece, log_piece, doc_piece, prev_doc):
-    cumulative = jnp.cumsum(log_piece, axis=0)
+def running_sum(log_seq):
+    rows = log_seq.shape[1]
+    lower = jnp.tril(jnp.ones((rows, rows), jnp.float32))
+    return jnp.einsum("ts,bsh->bth", lower, log_seq, precision=lax.Precision.HIGHEST)
+
+
+def piece_carry(xs_piece, b_piece, step_piece, cumulative, doc_piece, prev_doc):
     at_end = (doc_piece == doc_piece[-1])[:, None]
     weights = jnp.where(at_end, jnp.exp(cumulative[-1][None, :] - cumulative), 0.0) * step_piece
     states = jnp.einsum("qh,qhp,qn->hpn", weights, xs_piece, b_piece, precision=TOP_PRECISION)
@@ -116,10 +115,9 @@
 
 
 def piece_output(
-    xs_piece, b_piece, c_piece, step_piece, log_piece, doc_piece, prev_doc, carried, skip_scale
+    xs_piece, b_piece, c_piece, step_piece, cumulative, doc_piece, prev_doc, carried, skip_scale
 ):
-    cumulative = jnp.cumsum(log_piece, axis=0)
-    local_rows = log_piece.shape[0]
+    local_rows = cumulative.shape[0]
     row_index = lax.broadcasted_iota(jnp.int32, (local_rows, local_rows), 0)
     col_index = lax.broadcasted_iota(jnp.int32, (local_rows, local_rows), 1)
     linked = (row_index >= col_index) & (doc_piece[:, None] == doc_piece[None, :])
@@ -135,7 +133,7 @@
     return result + entering[:, :, None] * from_state + skip_scale[None, :, None] * xs_piece
 
 
-def score_block(query_row_block, keyvalue_rows, doc_query, doc_keys, query_places):
+def score_block(query_row_block, keyvalue_rows, doc_query, doc_keys, query_places, key_places):
     local_rows = query_row_block.shape[0]
     local_keys = keyvalue_rows.shape[0]
     key_span_width = KEYVALUE_HEADS * HEAD_SIZE
@@ -146,17 +144,17 @@
     score_matrix = jnp.einsum(
         "lbon,ybn->boly", query_head_rows, key_head_rows, preferred_element_type=jnp.float32
     ) * HEAD_SIZE ** (-0.5)
-    allowed = (query_places[:, None] >= jnp.arange(local_keys)[None, :]) & (
+    allowed = (query_places[:, None] >= key_places[None, :]) & (
         doc_query[:, None] == doc_keys[None, :]
     )
     return jnp.where(allowed[None, None], score_matrix, -1e30)
 
 
-def attend_forward(query_row_block, keyvalue_rows, doc_query, doc_keys, query_places):
+def attend_forward(query_row_block, keyvalue_rows, doc_query, doc_keys, query_places, key_places):
     local_rows = query_row_block.shape[0]
     local_keys = keyvalue_rows.shape[0]
     key_span_width = KEYVALUE_HEADS * HEAD_SIZE
-    masked = score_block(query_row_block, keyvalue_rows, doc_query, doc_keys, query_places)
+    masked = score_block(query_row_block, keyvalue_rows, doc_query, doc_keys, query_places, key_places)
     row_peak = jnp.max(masked, axis=-1, keepdims=True)
     exp_scores = jnp.exp(masked - row_peak)
     row_total = jnp.sum(exp_scores, axis=-1, keepdims=True)
@@ -174,12 +172,12 @@
 
 
 def attend_backward(
-    query_row_block, keyvalue_rows, doc_query, doc_keys, query_places, log_norm, mixed_gradient
+    query_row_block, keyvalue_rows, doc_query, doc_keys, query_places, key_places, log_norm, mixed_gradient
 ):
     local_rows = query_row_block.shape[0]
     local_keys = keyvalue_rows.shape[0]
     key_span_width = KEYVALUE_HEADS * HEAD_SIZE
-    masked = score_block(query_row_block, keyvalue_rows, doc_query, doc_keys, query_places)
+    masked = score_block(query_row_block, keyvalue_rows, doc_query, doc_keys, query_places, key_places)
     softmax_row_block = jnp.exp(masked - log_norm)
     query_head_rows = query_row_block.reshape(
         local_rows, KEYVALUE_HEADS, QUERY_HEADS // KEYVALUE_HEADS, HEAD_SIZE
@@ -303,6 +301,13 @@
     inv_one = lax.rsqrt(jnp.mean(flat_rows * flat_rows, axis=-1, keepdims=True) + EPSILON)
     gain_first = gain_one.astype(jnp.float32)
     normed = (flat_rows * inv_one * gain_first).astype(jnp.bfloat16)
+
+    def pieces(grads):
+        return [
+            product_tn(normed, grads[:, at : at + model_width]).astype(jnp.bfloat16)
+            for at in range(0, grads.shape[1], model_width)
+        ]
+
     main_raw = product(normed, main_full)
     at_query = width_gate + width_input
     gate_pre = main_raw[:, :width_gate]
@@ -340,12 +345,13 @@
     log_decay = -steps_dt * rates[None, :]
     step_seq = steps_dt.reshape(seq_count, piece_len, heads_ssm)
     log_seq = log_decay.reshape(seq_count, piece_len, heads_ssm)
+    sums_seq, sums_pull = jax.vjp(running_sum, log_seq)
 
     def carry_fn(xs_in, b_in, step_in, log_in):
         return jax.vmap(piece_carry)(xs_in, b_in, step_in, log_in, doc_own, prev_doc)
 
-    (decays, states), carry_pull = jax.vjp(carry_fn, xs_all, b_all, step_seq, log_seq)
-    entered = carried_states(decays, states, True)
+    (decays, states), carry_pull = jax.vjp(carry_fn, xs_all, b_all, step_seq, sums_seq)
+    entered = carried_states(decays, states, 1)
 
     def output_fn(xs_in, b_in, c_in, step_in, log_in, carried_in, skip_in):
         return jax.vmap(piece_output, in_axes=(0, 0, 0, 0, 0, 0, 0, 0, None))(
@@ -353,7 +359,7 @@
         )
 
     ssm_out, output_pull = jax.vjp(
-        output_fn, xs_all, b_all, c_all, step_seq, log_seq, entered, skip_scale
+        output_fn, xs_all, b_all, c_all, step_seq, sums_seq, entered, skip_scale
     )
     ssm_flat = ssm_out.reshape(-1, ssm_width)
     gate_act = jax.nn.silu(gate_pre)
@@ -369,12 +375,23 @@
     keyvalue_pairs = jnp.concatenate(
         [rotate(keyvalue_raw[:, :key_span_width], places), keyvalue_raw[:, key_span_width:]], axis=1
     ).astype(jnp.bfloat16)
-    kv_whole = lax.all_gather(
-        keyvalue_pairs.reshape(seq_count, piece_len, 2 * key_span_width), "seq", axis=1, tiled=True
+    kv_own = keyvalue_pairs.reshape(seq_count, piece_len, 2 * key_span_width)
+    seq_peers = lax.axis_size("seq")
+    kv_whole = jnp.concatenate(
+        [passed_along(kv_own, "seq", far) for far in range(seq_peers - 1, 0, -1)] + [kv_own],
+        axis=1,
+    )
+    before = (seq_peers - 1) * piece_len
+    key_places = first_row - before + jnp.arange(seq_peers * piece_len, dtype=jnp.int32)
+    doc_keys = lax.dynamic_slice_in_dim(
+        jnp.pad(documents, ((0, 0), (before, 0)), constant_values=-1),
+        first_row,
+        seq_peers * piece_len,
+        1,
     )
     query_seq = query_block.reshape(seq_count, piece_len, -1)
-    attn_mix, log_norm = jax.vmap(attend_forward, in_axes=(0, 0, 0, 0, None))(
-        query_seq, kv_whole, doc_own, documents, query_places
+    attn_mix, log_norm = jax.vmap(attend_forward, in_axes=(0, 0, 0, 0, None, None))(
+        query_seq, kv_whole, doc_own, doc_keys, query_places, key_places
     )
     attn_rows = attn_mix.reshape(seq_count * piece_len, -1).astype(jnp.bfloat16)
     attn_branch = product(attn_rows, attn_full)
@@ -404,11 +421,6 @@
     grad_normed_two = product_nt(grad_gate_up_rows, gate_up_full)
     grad_gain_two = jnp.sum(grad_normed_two * mixed_rows * inv_two, axis=0)
     mixed_gradient = grad_out + norm_back(mixed_rows, inv_two, grad_normed_two * gain_second)
-    ffn_pack = jnp.concatenate(
-        [part.reshape(devices, -1, model_width) for part in (*grad_pieces, grad_down)], axis=1
-    )
-    ffn_pack, mixed_gradient = lax.optimization_barrier((ffn_pack, mixed_gradient))
-    ffn_sums = lax.psum_scatter(ffn_pack, AXES, scatter_dimension=0)
     grad_branch = mixed_gradient.astype(jnp.bfloat16)
     grad_attn_w = product_tn(attn_rows, grad_branch).astype(jnp.bfloat16)
     grad_attn_rows = product_nt(grad_branch, attn_full).astype(jnp.bfloat16)
@@ -418,18 +430,30 @@
     grad_gated = norm_back(gated_rows, inv_mamba, grad_mamba_norm * gain_mamba.astype(jnp.float32))
     grad_ssm = grad_gated * gate_act
     grad_gate_pre = (grad_gated * ssm_flat * silu_slope(gate_pre)).astype(jnp.bfloat16)
-    grad_q_seq, grad_kv_whole = jax.vmap(attend_backward, in_axes=(0, 0, 0, 0, None, 0, 0))(
+    gate_pieces = pieces(grad_gate_pre)
+    early_parts = [*grad_pieces, *gate_pieces, grad_down, grad_mamba_out_w, grad_attn_w]
+    early_pack = jnp.concatenate(
+        [part.reshape(devices, -1, model_width) for part in early_parts], axis=1
+    )
+    early_pack, grad_attn_rows, grad_ssm = lax.optimization_barrier(
+        (early_pack, grad_attn_rows, grad_ssm)
+    )
+    early_sums = lax.psum_scatter(early_pack, AXES, scatter_dimension=0)
+    grad_q_seq, grad_kv_whole = jax.vmap(attend_backward, in_axes=(0, 0, 0, 0, None, None, 0, 0))(
         query_seq,
         kv_whole,
         doc_own,
-        documents,
+        doc_keys,
         query_places,
+        key_places,
         log_norm,
         grad_attn_rows.reshape(seq_count, piece_len, -1),
     )
-    grad_kv_own = lax.psum_scatter(
-        grad_kv_whole.astype(jnp.bfloat16), "seq", scatter_dimension=1, tiled=True
-    ).astype(jnp.float32)
+    grad_kv_own = grad_kv_whole[:, before:]
+    for far in range(1, seq_peers):
+        at = before - far * piece_len
+        sent = grad_kv_whole[:, at : at + piece_len].astype(jnp.bfloat16)
+        grad_kv_own = grad_kv_own + passed_along(sent, "seq", -far).astype(jnp.float32)
     grad_query_raw = rotate(grad_q_seq.reshape(seq_count * piece_len, -1), -places).astype(
         jnp.bfloat16
     )
@@ -441,10 +465,10 @@
     grad_xs_one, grad_b_one, grad_c_one, grad_step_one, grad_log_one, grad_entered, grad_skip = (
         output_pull(grad_ssm.reshape(ssm_out.shape))
     )
-    leaving = carried_states(decays, grad_entered, False)
+    leaving = carried_states(decays, grad_entered, -1)
     grad_decays = jnp.sum(leaving * entered, axis=(2, 3))
     grad_xs_two, grad_b_two, grad_step_two, grad_log_two = carry_pull((grad_decays, leaving))
-    grad_log = (grad_log_one + grad_log_two).reshape(-1, heads_ssm)
+    grad_log = sums_pull(grad_log_one + grad_log_two)[0].reshape(-1, heads_ssm)
     grad_steps = (grad_step_one + grad_step_two).reshape(-1, heads_ssm) - grad_log * rates[None, :]
     grad_decay_log = jnp.sum(grad_log * log_decay, axis=0)
     grad_step_sum = grad_steps * jax.nn.sigmoid(step_sum)
@@ -471,10 +495,8 @@
         [grad_gate_pre, grad_conv_in, grad_query_raw, grad_keyvalue_raw], axis=1
     )
     grad_normed = product_nt(grad_main, main_full) + product_nt(grad_step_raw, step_full)
-    main_pieces = [
-        product_tn(normed, grad_main[:, at : at + model_width]).astype(jnp.bfloat16)
-        for at in range(0, width_main, model_width)
-    ]
+    late_rows = grad_main[:, width_gate:]
+    main_pieces = pieces(late_rows)
     grad_step_w = product_tn(normed, grad_step_raw).astype(jnp.bfloat16)
     grad_gain_one = jnp.sum(grad_normed * flat_rows * inv_one, axis=0)
     grad_input = (
@@ -495,36 +517,36 @@
         jnp.pad(part, ((0, 0), (0, model_width - part.shape[1])))[:, None, :]
         for part in (grad_step_w.reshape(devices, -1), small_grads)
     ]
-    mixer_parts = [
-        part.reshape(devices, -1, model_width)
-        for part in (*main_pieces, grad_mamba_out_w, grad_attn_w)
-    ]
+    mixer_parts = [part.reshape(devices, -1, model_width) for part in main_pieces]
     spare = jnp.zeros((devices, 14, model_width), jnp.bfloat16)
     mixer_pack = jnp.concatenate([*mixer_parts, *small_rows, spare], axis=1)
     head_grads = jnp.stack([grad_step_bias, grad_decay_log, grad_skip])
     head_sums = jnp.sum(lax.all_gather(head_grads, AXES), axis=0)
     grad_step_bias, grad_decay_log, grad_skip = head_sums[0], head_sums[1], head_sums[2]
-    mixer_pack, ffn_sums = lax.optimization_barrier((mixer_pack, ffn_sums))
+    mixer_pack, early_sums = lax.optimization_barrier((mixer_pack, early_sums))
     mixer_sums = lax.psum_scatter(mixer_pack, AXES, scatter_dimension=0).astype(jnp.float32)
-    ffn_sums = ffn_sums.astype(jnp.float32)
-
-    def widened(rows, count):
-        return jnp.concatenate([rows[i * rows_one : (i + 1) * rows_one] for i in range(count)], 1)
-
-    ffn_count = len(grad_pieces)
-    grad_gate_up_w = widened(ffn_sums, ffn_count)
-    grad_down = ffn_sums[ffn_count * rows_one :]
-    main_count = len(main_pieces)
-    main_sums = widened(mixer_sums, main_count)
-    grad_gate_w = main_sums[:, :width_gate]
-    grad_input_w = main_sums[:, width_gate:at_query]
-    grad_query_w = main_sums[:, at_query : at_query + width_query]
-    grad_keyvalue_w = main_sums[:, at_query + width_query :]
-    at_row = main_count * rows_one
-    grad_mamba_out_w = mixer_sums[at_row : at_row + rows_output]
+    early_sums = early_sums.astype(jnp.float32)
+
+    def widened(rows, at, width):
+        parts = []
+        for spot in range(0, width, model_width):
+            wide = min(model_width, width - spot)
+            count = rows_one * wide // model_width
+            parts.append(rows[at : at + count].reshape(rows_one, wide))
+            at += count
+        return jnp.concatenate(parts, axis=1), at
+
+    grad_gate_up_w, at_row = widened(early_sums, 0, gate_up.shape[1])
+    grad_gate_w, at_row = widened(early_sums, at_row, width_gate)
+    grad_down = early_sums[at_row : at_row + down_weight.shape[0]]
+    at_row += down_weight.shape[0]
+    grad_mamba_out_w = early_sums[at_row : at_row + rows_output]
     at_row += rows_output
-    grad_attn_w = mixer_sums[at_row : at_row + attn_output.shape[0]]
-    at_row += attn_output.shape[0]
+    grad_attn_w = early_sums[at_row : at_row + attn_output.shape[0]]
+    late_sums, at_row = widened(mixer_sums, 0, width_main - width_gate)
+    grad_input_w = late_sums[:, :width_input]
+    grad_query_w = late_sums[:, width_input : width_input + width_query]
+    grad_keyvalue_w = late_sums[:, width_input + width_query :]
     grad_step_w = mixer_sums[at_row, : step_weight.size].reshape(step_weight.shape)
     small_out = []
     spot = 0

time: 948 us -> 825 us (0.87)
  waiting for transfers between devices: 362 us -> 241 us
  starting transfers between devices: 5.24 us -> 26.1 us
  local copies, waits for them, and re-layouts: 203 us -> 186 us
  other arithmetic: 129 us -> 116 us
  blocking collectives: 39.1 us -> 49 us
    all_gather x1, waiting for transfers between devices: 69.8 us -> 5.05 us  [local(): gate_up_full = lax.all_gather(third_pack, AXES, axis=0, tiled=True)]
    reduce_scatter x1, waiting for transfers between devices: 115 us -> 59.2 us  [local(): lax.psum_scatter(mixer_pack, AXES, scatter_dimension=0).astype(jnp.float32)]
    ppermute x2 -> x14, waiting for transfers between devices: 4.23 us -> 44.7 us  [passed_along(): return lax.ppermute(block, axis, route)]
    all_gather x1, waiting for transfers between devices: 32.9 us -> 0.01 us  [local(): second_full = lax.all_gather(second_pack, AXES, axis=0)]
    concatenate x1, local copies, waits for them, and re-layouts: 70.9 us -> 38.5 us  [local(): mixer_pack = jnp.concatenate([*mixer_parts, *small_rows, spare], axis=1)]
    ppermute x2 -> x14, starting transfers between devices: 4.62 us -> 25.7 us  [passed_along(): return lax.ppermute(block, axis, route)]
    all_gather x3 -> x0, waiting for transfers between devices: 13.5 us -> none  [the longest x2 13.5 us: pieces_of(): everything = lax.all_gather(packed, 'seq')]
    concatenate x1 -> x3, local copies, waits for them, and re-layouts: 2.43 us -> 15.3 us  [the longest x2 14.1 us: carried_states(): jnp.concatenate([states.astype(jnp.bfloat16).reshape(seqs, split, cols),...]
  transfers between devices with their start and end apart: 12 -> 20, of which waited for: 7 -> 8; matrix products, arithmetic and copies ran while one was open for 41% -> 46% of each run, Pallas kernels for 0% -> 0%
where the time goes in v2:
time: 825 us; the launch traced here: 814 us
  waiting for transfers between devices  241 us (29%)
  local copies, waits for them, and re-layouts  186 us (23%)
  matrix products  178 us (22%)
  other arithmetic  116 us (14%)
  blocking collectives  49 us (6%)
  starting transfers between devices  26.1 us (3%)
  between operations  17 us (2%)
    all_gather x1, waiting for transfers between devices, local(): first_full = lax.all_gather(first_pack, AXES, axis=0, tiled=True)  79.6 us
    reduce_scatter x1, waiting for transfers between devices, local(): lax.psum_scatter(mixer_pack, AXES, scatter_dimension=0).astype(jnp.float32)  59.2 us
    all_gather x1, waiting for transfers between devices, local(): down_full = lax.all_gather(fourth_pack, AXES, axis=0, tiled=True)  52.1 us
    all_gather x1, blocking collectives, local(): head_sums = jnp.sum(lax.all_gather(head_grads, AXES), axis=0)  49 us
    ppermute x14, waiting for transfers between devices, passed_along(): return lax.ppermute(block, axis, route)  44.7 us
    concatenate x1, local copies, waits for them, and re-layouts, local(): mixer_pack = jnp.concatenate([*mixer_parts, *small_rows, spare], axis=1)  38.5 us
    unnamed x347, local copies, waits for them, and re-layouts  38.1 us
    dot_general x6, matrix products, product(): return jnp.dot(left_side, right_side, preferred_element_type=jnp.float32)  33.5 us
  transfers between devices with their start and end apart: 20, of which 8 were waited for; matrix products, arithmetic and copies ran while one was open for 46% of the time, Pallas kernels for 0%

profile of v2, /device:TPU:0, one launch (start us, length us, event | category | flops | bytes accessed | tf_op | source)
XLA Modules:
  0.0 814.0 jit_solution(1927188790720458203)
XLA Ops:
  15.2 79.6 %all-gather.8.cloned.1.call-done = bf16[1024,4224]{1,0:T(8,128)(2,1)} async-done(((bf16[32,4224]{1,0:T(8,128)(2,1)}), bf16[1024,4224]{1,0:T(8,128)(2,1)}) %all-gather.8.cloned.1.call-update) | async-done | bytes 8650768 | tf_op jit(solution)/shard_map/all_gather | solution.py:268
  108.6 10.4 %fusion.189 = (bf16[512,4096]{1,0:T(8,128)(2,1)S(1)}, f32[512,4096]{1,0:T(8,128)}) fusion(bf16[512,1024]{1,0:T(8,128)(2,1)S(1)} %fusion.62, bf16[1024,4224]{1,0:T(8,128)(2,1)} %all-gather.8.cloned.1.call-done), kind=kOutput, calls=%fused_computation.384 | convolution fusion | flops 4297064448 | bytes 22020096 | tf_op jit(solution)/shard_map/dot_general | solution.py:46
  165.2 7.1 copy.493
  182.4 9.7 %maximum_maximum_fusion = bf16[2,1024,256]{1,0,2:T(2,128)(2,1)S(1)} fusion(bf16[2,256,128]{1,0,2:T(2,128)(2,1)S(1)} %copy.499, bf16[2,256,128]{1,0,2:T(2,128)(2,1)S(1)} %copy-done.69, bf16[2,256,256]{1,0,2:T(2,128)(2,1)} %collective-permute-done.6, bf16[2,256,256]{1,0,2:T(2,128)(2,1)} %collective-permute-done.5, bf16[2,256,256]{1,0,2:T(2,128)(2,1)} %collective-permute-done.4), kind=kLoop, calls=%fused_computation.180 | loop fusion | flops 5242880 | bytes 2097152 | tf_op jit(solution)/shard_map/concatenate | solution.py:380
  193.1 7.3 fusion.190
  200.4 8.0 fusion.3
  208.4 7.4 fusion.92
  257.7 11.5 %fusion.191 = f32[512,4096]{1,0:T(8,128)} fusion(bf16[512,1024]{1,0:T(8,128)(2,1)} %multiply_convert_fusion.4, bf16[1024,4096]{1,0:T(8,128)(2,1)} %all-gather.10.cloned.1.call-done), kind=kOutput, calls=%fused_computation.386 | convolution fusion | flops 4294967296 | bytes 17825792 | tf_op jit(solution)/shard_map/dot_general | solution.py:46
  269.2 52.1 %all-gather.12.cloned.1.call-done = bf16[2048,1024]{1,0:T(8,128)(2,1)} async-done(((bf16[64,1024]{1,0:T(8,128)(2,1)}), bf16[2048,1024]{1,0:T(8,128)(2,1)}) %all-gather.12.cloned.1.call-update) | async-done | bytes 4194320 | tf_op jit(solution)/shard_map/all_gather | solution.py:274
  321.3 8.8 %fusion.39 = (bf16[512,2048]{1,0:T(8,128)(2,1)S(1)}, bf16[512,2048]{1,0:T(8,128)(2,1)S(1)}, bf16[512,2048]{1,0:T(8,128)(2,1)S(1)}) fusion(f32[512,4096]{1,0:T(8,128)} %fusion.191, bf16[2048,1024]{1,0:T(8,128)(2,1)} %all-gather.12.cloned.1.call-done, bf16[512,1024]{1,0:T(8,128)(2,1)} %bitcast.377), kind=kOutput, calls=%fused_computation.48 | convolution fusion | flops 2163212288 | bytes 19922944 | tf_op jit(solution)/shard_map/dot_general | solution.py:56
  330.2 9.4 %multiply_reduce_fusion.10 = (bf16[1024]{0:T(1024)(128)(2,1)S(1)}, f32[512]{0:T(512)S(1)}, f32[512,1024]{1,0:T(8,128)S(1)}) fusion(f32[512,1024]{1,0:T(8,128)S(1)} %copy-done.15, f32[512]{0:T(512)S(1)} %get-tuple-element.264, f32[1024]{0:T(1024)S(1)} %copy-done.129, bf16[1024,4096]{1,0:T(8,128)(2,1)} %all-gather.10.cloned.1.call-done, ...), kind=kOutput, calls=%fused_computation.122 | convolution fusion | flops 4306500096 | bytes 16787456 | tf_op jit(solution)/shard_map/dot_general | solution.py:56
  407.6 7.1 copy.512
  422.0 11.7 %fusion.21 = (f32[2,24,256]{2,1,0:T(8,128)S(1)}, f32[2,24,256]{2,1,0:T(8,128)S(1)}, f32[2,24,256]{2,1,0:T(8,128)S(1)}, bf16[2,256,256]{2,1,0:T(8,128)(2,1)}) fusion(f32[2,24,256]{2,1,0:T(8,128)S(1)} %copy-done.127, f32[2,256,256]{2,1,0:T(8,128)} %fusion.142, f32[2,24,256]{2,1,0:T(8,128)S(1)} %copy-done.123, pred[2,256,256]{2,1,0:T(8,128)(4,1)S(1)} %copy-done.102, ...), kind=kOutput, calls=%fused_computation.28 | convolution fusion | flops 449671168 | bytes 5881856 | tf_op jit(solution)/shard_map/transpose(jvp(vmap(hts,shp->thp)))/dot_general | solution.py:130
  439.2 15.1 %fusion = (f32[2,2,4,256]{3,2,1,0:T(4,128)S(1)}, f32[2,2,1024,256,4]{3,2,4,1,0:T(8,128)}) fusion(f32[2,2,4,256,1024]{3,4,2,1,0:T(8,128)} %get-tuple-element.276, f32[2,2,4,256]{3,2,1,0:T(4,128)S(1)} %bitcast.384, bf16[2,1024,2,64,1]{1,3,4,2,0:T(8,128)(2,1)S(1)} %bitcast.358, bf16[2,256,2,4,64]{1,4,3,2,0:T(8,128)(2,1)S(1)} %copy.525), kind=kOutput, calls=%fused_computation.2 | convolution fusion | flops 549449728 | bytes 34635776 | tf_op jit(solution)/shard_map/vmap(lbon,ybn->boly)/dot_general | solution.py:192
  455.9 8.1 fusion.2
  477.2 7.4 fusion.12
  491.6 9.5 %collective-permute-done.11 = bf16[2,256,256]{1,2,0:T(8,128)(2,1)S(1)} collective-permute-done((bf16[2,256,256]{1,2,0:T(8,128)(2,1)S(1)}, bf16[2,256,256]{1,2,0:T(8,128)(2,1)S(1)}, u32[]{:S(2)}, u32[]{:S(2)}) %collective-permute-start.11) | collective-permute-done | bytes 262176 | tf_op jit(solution)/shard_map/ppermute | solution.py:23
  502.3 13.5 %collective-permute-done.13 = bf16[2,256,256]{1,2,0:T(8,128)(2,1)S(1)} collective-permute-done((bf16[2,256,256]{1,2,0:T(8,128)(2,1)S(1)}, bf16[2,256,256]{1,2,0:T(8,128)(2,1)S(1)}, u32[]{:S(2)}, u32[]{:S(2)}) %collective-permute-start.13) | collective-permute-done | bytes 262176 | tf_op jit(solution)/shard_map/ppermute | solution.py:23
  523.4 17.4 %collective-permute-done.7 = bf16[2,1552,128]{2,0,1:T(2,128)(2,1)} collective-permute-done((bf16[2,1552,128]{2,0,1:T(2,128)(2,1)}, bf16[2,1552,128]{2,0,1:T(2,128)(2,1)}, u32[]{:S(2)}, u32[]{:S(2)}) %collective-permute-start.7) | collective-permute-done | bytes 794656 | tf_op jit(solution)/shard_map/ppermute | solution.py:23
  565.6 7.1 multiply_reduce_fusion.5
  579.6 9.7 %fusion.73 = f32[2,1536,128]{2,0,1:T(2,128)S(1)} fusion(f32[2,1536,128]{2,1,0:T(8,128)S(1)} %copy-done.20, f32[2,1536]{0,1:T(8,128)S(1)} %bitcast.351, f32[2,1552,128]{2,0,1:T(2,128)S(1)} %copy-done.34), kind=kLoop, calls=%fused_computation.140 | loop fusion | flops 786432 | bytes 4730880 | tf_op jit(solution)/shard_map/add | solution.py:40
  633.9 38.5 %concatenate.126 = bf16[32,96,1024]{2,1,0:T(8,128)(2,1)} concatenate(bf16[32,32,1024]{2,1,0:T(8,128)(2,1)} %bitcast.360, bf16[32,32,1024]{2,1,0:T(8,128)(2,1)} %bitcast.359, bf16[32,16,1024]{2,1,0:T(8,128)(2,1)} %reshape.699, bf16[32,1,1024]{2,1,0:T(2,128)(2,1)S(1)} %copy.553, bf16[32,1,1024]{2,1,0:T(2,128)(2,1)S(1)} %copy-done.85, bf16[32,14,1024]{2,1,0:T(8,128)(2,1)S(1)} %broadcast_in_dim.232), dimensions={1} | concatenate | bytes 12582912 | tf_op jit(solution)/shard_map/concatenate | solution.py:522
  683.3 49.0 %all-gather.2 = f32[32,3,24]{2,1,0:T(4,128)S(1)} all-gather(f32[1,3,24]{2,1,0:T(4,128)S(1)} %maximum_bitcast_fusion), channel_id=3, replica_groups=mesh['seq'=4,'dp'=8] {'seq','dp'}, dimensions={0}, use_global_device_ids=true | all-gather | bytes 9504 | tf_op jit(solution)/shard_map/all_gather | solution.py:524
  740.8 59.2 %reduce-scatter.5.cloned.1.call-done = bf16[1,96,1024]{2,1,0:T(8,128)(2,1)} async-done(((bf16[32,96,1024]{2,1,0:T(8,128)(2,1)}), bf16[1,96,1024]{2,1,0:T(8,128)(2,1)}) %reduce-scatter.5.cloned.1.call-update) | async-done | bytes 196624 | tf_op jit(solution)/shard_map/reduce_scatter | solution.py:527
  (643 shorter events, 332.5 us)
Async XLA Ops:
  7.2 101.1 %copy-start.9 = (bf16[2,256,1024]{2,1,0:T(8,128)(2,1)S(1)}, bf16[2,256,1024]{2,1,0:T(8,128)(2,1)}, u32[]{:S(2)}) copy-start(bf16[2,256,1024]{2,1,0:T(8,128)(2,1)} %param.20) | copy-start | bytes 3145732
  7.2 87.6 %all-gather.8.cloned.1.call-start = ((), (), s32[]{:S(2)}) async-start(), calls=%async_computation.2 | async-start | bytes 8921088 | tf_op jit(solution)/shard_map/all_gather | solution.py:268
  13.5 229.0 %all-gather.14.cloned.1.call-start = ((), (), s32[]{:S(2)}) async-start(), calls=%async_computation.7 | async-start | bytes 4325376 | tf_op jit(solution)/shard_map/all_gather | solution.py:272
  94.8 162.9 %all-gather.10.cloned.1.call-start = ((), (), s32[]{:S(2)}) async-start(), calls=%async_computation.3 | async-start | bytes 8650752 | tf_op jit(solution)/shard_map/all_gather | solution.py:273
  95.5 225.8 %all-gather.12.cloned.1.call-start = ((), (), s32[]{:S(2)}) async-start(), calls=%async_computation.4 | async-start | bytes 4325376 | tf_op jit(solution)/shard_map/all_gather | solution.py:274
  122.9 57.6 %collective-permute-start.6 = (bf16[2,256,256]{1,0,2:T(2,128)(2,1)}, bf16[2,256,256]{1,0,2:T(2,128)(2,1)}, u32[]{:S(2)}, u32[]{:S(2)}) collective-permute-start(bf16[2,256,256]{1,0,2:T(2,128)(2,1)} %pad_maximum_fusion.12), channel_id=1, source_target_pairs={{0,8},{8,16},{16,24},{1,9},{9,17},{17,25},{2,10},{10,18},{18,26},{... | collective-permute-start | bytes 786440 | tf_op jit(solution)/shard_map/ppermute | solution.py:23
  126.9 55.4 %collective-permute-start.5 = (bf16[2,256,256]{1,0,2:T(2,128)(2,1)}, bf16[2,256,256]{1,0,2:T(2,128)(2,1)}, u32[]{:S(2)}, u32[]{:S(2)}) collective-permute-start(bf16[2,256,256]{1,0,2:T(2,128)(2,1)} %pad_maximum_fusion.12), channel_id=1, source_target_pairs={{0,16},{8,24},{1,17},{9,25},{2,18},{10,26},{3,19},{11,27},{4,20},{... | collective-permute-start | bytes 786440 | tf_op jit(solution)/shard_map/ppermute | solution.py:23
  129.4 52.9 %collective-permute-start.4 = (bf16[2,256,256]{1,0,2:T(2,128)(2,1)}, bf16[2,256,256]{1,0,2:T(2,128)(2,1)}, u32[]{:S(2)}, u32[]{:S(2)}) collective-permute-start(bf16[2,256,256]{1,0,2:T(2,128)(2,1)} %pad_maximum_fusion.12), channel_id=1, source_target_pairs={{0,24},{1,25},{2,26},{3,27},{4,28},{5,29},{6,30},{7,31}} | collective-permute-start | bytes 786440 | tf_op jit(solution)/shard_map/ppermute | solution.py:23
  142.4 10.2 %collective-permute-start = (bf16[2,3,1792]{2,1,0:T(4,128)(2,1)}, bf16[2,3,1792]{2,1,0:T(4,128)(2,1)}, u32[]{:S(2)}, u32[]{:S(2)}) collective-permute-start(bf16[2,3,1792]{2,1,0:T(4,128)(2,1)} %slice.473), channel_id=1, source_target_pairs={{0,8},{8,16},{16,24},{1,9},{9,17},{17,25},{2,10},{10,18},{18,26},{... | collective-permute-start | bytes 64520 | tf_op jit(solution)/shard_map/ppermute | solution.py:23
  150.4 522.0 %reduce-scatter.3.cloned.1.call-start = ((), (), s32[]{:S(2)}) async-start(), calls=%async_computation.5 | async-start | bytes 20545536 | tf_op jit(solution)/shard_map/reduce_scatter | solution.py:441
  158.3 63.0 %copy-start.13 = (bf16[2,256,1792]{2,1,0:T(8,128)(2,1)}, bf16[2,256,1792]{2,1,0:T(8,128)(2,1)S(1)}, u32[]{:S(2)}) copy-start(bf16[2,256,1792]{2,1,0:T(8,128)(2,1)S(1)} %get-tuple-element.204) | copy-start | bytes 5505028
  172.3 46.9 %collective-permute-start.3 = (bf16[2,1552,128]{2,1,0:T(8,128)(2,1)}, bf16[2,1552,128]{2,1,0:T(8,128)(2,1)}, u32[]{:S(2)}, u32[]{:S(2)}) collective-permute-start(bf16[2,1552,128]{2,1,0:T(8,128)(2,1)} %pad_maximum_fusion.2), channel_id=1, source_target_pairs={{0,24},{1,25},{2,26},{3,27},{4,28},{5,29},{6,30},{7,31}} | collective-permute-start | bytes 2383880 | tf_op jit(solution)/shard_map/ppermute | solution.py:23
  174.5 44.2 %collective-permute-start.2 = (bf16[2,1552,128]{2,1,0:T(8,128)(2,1)}, bf16[2,1552,128]{2,1,0:T(8,128)(2,1)S(1)}, u32[]{:S(2)}, u32[]{:S(2)}) collective-permute-start(bf16[2,1552,128]{2,1,0:T(8,128)(2,1)} %pad_maximum_fusion.2), channel_id=1, source_target_pairs={{0,16},{8,24},{1,17},{9,25},{2,18},{10,26},{3,19},{11,27},{4,20},{... | collective-permute-start | bytes 2383880 | tf_op jit(solution)/shard_map/ppermute | solution.py:23
  180.5 36.8 %collective-permute-start.1 = (bf16[2,1552,128]{2,0,1:T(2,128)(2,1)}, bf16[2,1552,128]{2,0,1:T(2,128)(2,1)S(1)}, u32[]{:S(2)}, u32[]{:S(2)}) collective-permute-start(bf16[2,1552,128]{2,0,1:T(2,128)(2,1)} %copy.493), channel_id=1, source_target_pairs={{0,8},{8,16},{16,24},{1,9},{9,17},{17,25},{2,10},{10,18},{18,26},{... | collective-permute-start | bytes 2383880 | tf_op jit(solution)/shard_map/ppermute | solution.py:23
  397.0 403.0 %reduce-scatter.5.cloned.1.call-start = ((), (), s32[]{:S(2)}) async-start(), calls=%async_computation.6 | async-start | bytes 6488064 | tf_op jit(solution)/shard_map/reduce_scatter | solution.py:527
  414.7 134.1 %collective-permute-start.9 = (bf16[2,1552,128]{2,1,0:T(8,128)(2,1)}, bf16[2,1552,128]{2,1,0:T(8,128)(2,1)}, u32[]{:S(2)}, u32[]{:S(2)}) collective-permute-start(bf16[2,1552,128]{2,1,0:T(8,128)(2,1)} %pad_maximum_fusion.1), channel_id=1, source_target_pairs={{24,0},{25,1},{26,2},{27,3},{28,4},{29,5},{30,6},{31,7}} | collective-permute-start | bytes 2383880 | tf_op jit(solution)/shard_map/ppermute | solution.py:23
  416.0 129.3 %collective-permute-start.8 = (bf16[2,1552,128]{2,1,0:T(8,128)(2,1)}, bf16[2,1552,128]{2,1,0:T(8,128)(2,1)}, u32[]{:S(2)}, u32[]{:S(2)}) collective-permute-start(bf16[2,1552,128]{2,1,0:T(8,128)(2,1)} %pad_maximum_fusion.1), channel_id=1, source_target_pairs={{16,0},{24,8},{17,1},{25,9},{18,2},{26,10},{19,3},{27,11},{20,4},{... | collective-permute-start | bytes 2383880 | tf_op jit(solution)/shard_map/ppermute | solution.py:23
  484.9 16.2 %collective-permute-start.11 = (bf16[2,256,256]{1,2,0:T(8,128)(2,1)S(1)}, bf16[2,256,256]{1,2,0:T(8,128)(2,1)S(1)}, u32[]{:S(2)}, u32[]{:S(2)}) collective-permute-start(bf16[2,256,256]{1,2,0:T(8,128)(2,1)S(1)} %get-tuple-element.219), channel_id=1, source_target_pairs={{8,0},{16,8},{24,16},{9,1},{17,9},{25,17},{10,2},{18,10},{26,18},{... | collective-permute-start | bytes 786440 | tf_op jit(solution)/shard_map/ppermute | solution.py:23
  486.4 29.4 %collective-permute-start.13 = (bf16[2,256,256]{1,2,0:T(8,128)(2,1)S(1)}, bf16[2,256,256]{1,2,0:T(8,128)(2,1)S(1)}, u32[]{:S(2)}, u32[]{:S(2)}) collective-permute-start(bf16[2,256,256]{1,2,0:T(8,128)(2,1)S(1)} %get-tuple-element.220), channel_id=1, source_target_pairs={{24,0},{25,1},{26,2},{27,3},{28,4},{29,5},{30,6},{31,7}} | collective-permute-start | bytes 786440 | tf_op jit(solution)/shard_map/ppermute | solution.py:23
  487.7 28.1 %collective-permute-start.12 = (bf16[2,256,256]{1,2,0:T(8,128)(2,1)S(1)}, bf16[2,256,256]{1,2,0:T(8,128)(2,1)S(1)}, u32[]{:S(2)}, u32[]{:S(2)}) collective-permute-start(bf16[2,256,256]{1,2,0:T(8,128)(2,1)S(1)} %get-tuple-element.221), channel_id=1, source_target_pairs={{16,0},{24,8},{17,1},{25,9},{18,2},{26,10},{19,3},{27,11},{20,4},{... | collective-permute-start | bytes 786440 | tf_op jit(solution)/shard_map/ppermute | solution.py:23
  501.1 39.7 %collective-permute-start.7 = (bf16[2,1552,128]{2,0,1:T(2,128)(2,1)}, bf16[2,1552,128]{2,0,1:T(2,128)(2,1)}, u32[]{:S(2)}, u32[]{:S(2)}) collective-permute-start(bf16[2,1552,128]{2,0,1:T(2,128)(2,1)} %copy.512), channel_id=1, source_target_pairs={{8,0},{16,8},{24,16},{9,1},{17,9},{25,17},{10,2},{18,10},{26,18},{... | collective-permute-start | bytes 2383880 | tf_op jit(solution)/shard_map/ppermute | solution.py:23
  602.9 6.7 collective-permute-start.10
  676.4 56.6 %copy-start.146 = (f32[512]{0:T(512)S(1)}, f32[512]{0:T(512)}, u32[]{:S(2)}) copy-start(f32[512]{0:T(512)} %get-tuple-element.184) | copy-start | bytes 6148
  676.4 56.6 %copy-start.12 = (bf16[2,256,1024]{2,1,0:T(8,128)(2,1)S(1)}, bf16[2,256,1024]{2,1,0:T(8,128)(2,1)}, u32[]{:S(2)}) copy-start(bf16[2,256,1024]{2,1,0:T(8,128)(2,1)} %param.20) | copy-start | bytes 3145732
  (160 other events, 1225.0 us)
Sparse Core Ops, SparseCore 0:
  13.6 81.0 all-gather.7
  98.3 62.1 all-gather.13
  163.6 94.1 all-gather.9
  260.6 60.6 all-gather.11
  397.1 217.9 reduce-scatter.2
  672.6 127.2 reduce-scatter.4
